TPU v7x, 256 devices: a whole 4x4x8 slice. The times are simulated.
256 devices in a mesh: phase: 8 (over z), ctx: 16 (over x, y), tp: 2 (over core).
Axes of the slice: x: 4, y: 4, z: 8, core: 2. Of those that a mesh axis runs over, the one named last changes fastest.
Arguments:
- hidden_in: bfloat16 [1, 2048, 3072], P(None, 'ctx', 'tp'), may hold values from -48 to 48
- qkv_weight: bfloat16 [8, 32, 96, 288], P('phase', 'tp'), may hold values from -0.625 to 0.625
- log_decay: float32 [8, 1, 2048, 32], P('phase', None, 'ctx', 'tp'), may hold values from -0.6 to 0
- lengths: int32 [1, 4], replicated, may hold values from 1 to 1536, 2048 in all within a row
- out_mantissa: bfloat16 [8, 3072, 3072], P('phase', 'ctx', 'tp'), may hold values from -0.109375 to 0.109375
- out_exponent: int32 [8, 32, 32], P('phase', None, 'tp'), may hold values from -3 to 1
Outputs:
- outputs: bfloat16 [8, 1, 2048, 3072], P('phase', None, 'ctx', 'tp')
Inputs may be any that keep to these rules, and one draw needn't show every extreme that they name: lengths[m] lists the 4 prompt lengths packed in micro-batch m in order; they sum to 2048 and the largest is exactly 1536.
All inputs are finite; a program needn't handle non-finite values.
Results may differ from a plain program's by a relative error of at most 0.034.
Values may be sent and summed in bfloat16 or wider, within the bound.
A program may use at most 128 MiB of HBM per device.

v0:
```python
import jax
import jax.numpy as jnp
from jax import lax
from jax.sharding import PartitionSpec as P

epsilon = 1e-05


def carried_in(array, axis, join, neutral):
    place = lax.axis_index(axis)
    gathered = jax.tree.map(
        lambda a, kind: lax.all_gather(a.astype(kind), axis), array, (jnp.bfloat16, jnp.bfloat16)
    )
    state = jax.tree.map(lambda a, e: jnp.zeros_like(a) + jnp.asarray(e, a.dtype), array, neutral)

    def one(lap, state):
        return join(
            state,
            jax.tree.map(
                lambda a, own: lax.dynamic_index_in_dim(a, lap, 0, False).astype(own.dtype),
                gathered,
                array,
            ),
        )

    return lax.fori_loop(0, place, one, state)


def from_behind(block, axis, distance):
    devices = range(lax.axis_size(axis))
    route = [(i - distance, i) for i in devices if i - distance in devices]
    return lax.ppermute(block, axis, route)


def dequantize(mantissa, exponent, head_size):
    scale = jnp.exp2(exponent.astype(jnp.float32))
    blocks = mantissa.astype(jnp.float32).reshape(
        exponent.shape[0], head_size, exponent.shape[1], head_size
    )
    return (blocks * scale[:, None, :, None]).reshape(mantissa.shape).astype(jnp.bfloat16)


def combine_states(earlier, later):
    return (earlier[0] * later[0], later[0][:, None, None] * earlier[1] + later[1])


def inner_term(query_rows, key_rows, value_rows, decayed, segment):
    count = segment.shape[0]
    places = jnp.arange(count)
    allowed = (places[None, :] <= places[:, None]) & (segment[None, :] == segment[:, None])
    spread = decayed[:, :, None] - decayed[:, None, :]
    multiplier = jnp.exp(jnp.where(allowed[None], spread, -1e30))
    scores = jnp.einsum("hid,hjd->hij", query_rows, key_rows, preferred_element_type=jnp.float32)
    weights = (scores * multiplier).astype(jnp.bfloat16)
    return jnp.einsum("hij,hjd->hid", weights, value_rows, preferred_element_type=jnp.float32)


def state_terms(query_rows, key_rows, value_rows, decayed, segment, before):
    final = decayed[:, -1]
    in_last = (segment == segment[-1]).astype(jnp.float32)
    key_scale = jnp.exp(final[:, None] - decayed) * in_last[None, :]
    keyed = (key_rows.astype(jnp.float32) * key_scale[:, :, None]).astype(jnp.bfloat16)
    own = jnp.einsum("hjd,hje->hde", keyed, value_rows, preferred_element_type=jnp.float32)
    carry_on = jnp.where(segment[-1] == before, jnp.exp(final), jnp.zeros_like(final))
    continues = (segment == before).astype(jnp.float32)
    query_scale = jnp.exp(decayed) * continues[None, :]
    queried = (query_rows.astype(jnp.float32) * query_scale[:, :, None]).astype(jnp.bfloat16)
    return (own, carry_on, queried)


def finish(inner, queried, state):
    attended = inner + jnp.einsum(
        "hid,hde->hie", queried, state.astype(jnp.bfloat16), preferred_element_type=jnp.float32
    )
    scale = lax.rsqrt(jnp.mean(attended * attended, axis=2, keepdims=True) + epsilon)
    normed = (attended * scale).astype(jnp.bfloat16)
    return normed.transpose(1, 0, 2).reshape(normed.shape[1], -1)


def pass_states(carry_on, own):
    identity = (jnp.ones_like(carry_on), jnp.zeros_like(own))
    return carried_in((carry_on, own), "ctx", combine_states, identity)


def shards(hidden_in, qkv_weight, log_decay, lengths, out_mantissa, out_exponent):
    micro, rows, half = hidden_in.shape
    heads_here = qkv_weight.shape[1]
    head_size = qkv_weight.shape[2]
    phases = lax.axis_size("phase")
    phase_index = lax.axis_index("phase")
    ctx_index = lax.axis_index("ctx")
    mantissa_all = lax.all_gather(out_mantissa[0], "ctx", axis=0, tiled=True)
    width = mantissa_all.shape[0]
    out_weight = dequantize(mantissa_all, out_exponent[0], head_size)
    positions = ctx_index * rows + jnp.arange(rows, dtype=jnp.int32)

    def add_heads(piece):
        return jnp.dot(piece, out_weight, preferred_element_type=jnp.float32)

    def run_turn(turn_index, incoming, outputs):
        offset = turn_index - phase_index
        active = (offset >= 0) & (offset < micro)
        micro_index = jnp.clip(offset, 0, micro - 1)
        first = lax.dynamic_index_in_dim(hidden_in, micro_index, 0, keepdims=False)
        current = jnp.where(phase_index == 0, first, incoming).astype(jnp.float32)
        squares = lax.psum(jnp.sum(current * current, axis=1), "tp")
        inverse = lax.rsqrt(squares / width + epsilon)
        normed = (current * inverse[:, None]).astype(jnp.bfloat16)
        project = jnp.einsum(
            "rhd,hde->hre",
            normed.reshape(rows, heads_here, head_size),
            qkv_weight[0],
            preferred_element_type=jnp.float32,
        )
        query_rows = jax.nn.silu(project[:, :, :head_size]).astype(jnp.bfloat16)
        key_rows = jax.nn.silu(project[:, :, head_size : 2 * head_size]).astype(jnp.bfloat16)
        value_rows = project[:, :, 2 * head_size :].astype(jnp.bfloat16)
        lengths_row = lax.dynamic_index_in_dim(lengths, micro_index, 0, keepdims=False)
        ends = jnp.cumsum(lengths_row)[:-1]
        segment = jnp.sum((positions[:, None] >= ends[None, :]).astype(jnp.int32), axis=1)
        earlier_count = jnp.sum((positions[0] - 1 >= ends).astype(jnp.int32))
        before = jnp.where(ctx_index == 0, -1, earlier_count)
        decay_rows = lax.dynamic_index_in_dim(log_decay[0], micro_index, 0, keepdims=False)
        decayed = jnp.cumsum(decay_rows.T, axis=1)
        inner = inner_term(query_rows, key_rows, value_rows, decayed, segment)
        own, carry_on, queried = state_terms(
            query_rows, key_rows, value_rows, decayed, segment, before
        )
        carry_in, state = pass_states(carry_on, own)
        attended = finish(inner, queried, state)
        mixed = add_heads(lax.all_gather(attended, "tp", axis=1, tiled=True))
        result = (current + mixed).astype(jnp.bfloat16)
        previous = lax.dynamic_index_in_dim(outputs, micro_index, 0, keepdims=False)
        outputs = lax.dynamic_update_index_in_dim(
            outputs, jnp.where(active, result, previous), micro_index, 0
        )
        return (result, outputs)

    def advance(turn_index, carried):
        result, outputs = run_turn(turn_index, carried[0], carried[1])
        return (from_behind(result, "phase", 1), outputs)

    turns = micro + phases - 1
    initial = (jnp.zeros((rows, half), jnp.bfloat16), jnp.zeros((micro, rows, half), jnp.bfloat16))
    incoming, outputs = lax.fori_loop(0, turns - 1, advance, initial)
    final_rows, outputs = run_turn(turns - 1, incoming, outputs)
    return outputs[None]


def solution(mesh):
    in_specs = (
        P(None, "ctx", "tp"),
        P("phase", "tp", None, None),
        P("phase", None, "ctx", "tp"),
        P(),
        P("phase", "ctx", "tp"),
        P("phase", None, "tp"),
    )
    out_specs = P("phase", None, "ctx", "tp")
    return jax.shard_map(shards, mesh=mesh, in_specs=in_specs, out_specs=out_specs, check_vma=False)
```

profile of v0, /device:TPU:31, one launch (start us, length us, event | category | flops | bytes accessed | tf_op | source)
XLA Modules:
  0.0 1106.8 jit_solution(14081611705850923076)
XLA Ops:
  10.7 10.0 mul.309
  20.7 26.7 %mul.310 = f32[3072,1536]{1,0:T(8,128)} reshape(f32[32,96,16,96]{3,2,1,0:T(8,128)} %mul.309) | data formatting | bytes 37748736 | tf_op jit(solution)/shard_map/mul | solution.py:40
  51.9 39.5 %all-gather.15.cloned.1.call-done = bf16[1,3072,1536]{2,1,0:T(8,128)(2,1)} async-done(((bf16[1,192,1536]{2,1,0:T(8,128)(2,1)}), bf16[1,3072,1536]{2,1,0:T(8,128)(2,1)}) %all-gather.15.cloned.1.call-update) | async-done | bytes 9437200 | tf_op jit(solution)/shard_map/all_gather | solution.py:92
  91.4 14.1 %fusion.26 = bf16[3072,1536]{1,0:T(8,128)(2,1)} fusion(f32[3072,1536]{1,0:T(8,128)} %mul.310, bf16[1,3072,1536]{2,1,0:T(8,128)(2,1)} %all-gather.15.cloned.1.call-done), kind=kLoop, calls=%fused_computation.59 | loop fusion | flops 14155776 | bytes 37748736 | tf_op jit(solution)/shard_map/convert_element_type | solution.py:40
  106.3 889.5 %while.59 = (s32[]{:T(128)}, bf16[128,1536]{1,0:T(8,128)(2,1)S(1)}, bf16[1,128,1536]{2,1,0:T(8,128)(2,1)}, pred[]{:T(512)}, bf16[1,128,1536]{2,1,0:T(8,128)(2,1)...) while((s32[]{:T(128)}, bf16[128,1536]{1,0:T(8,128)(2,1)S(1)}, ...), condition=%wide.region_10.11_spmd.clone, body=%wide.region_2.10_spmd.clone.sunk | while | flops 1507862400 | bytes 52832948 | solution.py:145
  117.2 14.7 %all-gather.9 = bf16[16,1,16]{2,1,0:T(2,128)(2,1)S(1)} all-gather(bf16[1,1,16]{2,1,0:T(2,128)(2,1)S(1)} %fusion.82), channel_id=1, replica_groups=mesh['phase'=8,'ctx'=16,'tp'=2] {'ctx'}, dimensions={0}, use_global_device_ids=true | all-gather | bytes 544 | tf_op jit(solution)/shard_map/while/body/eval_jaxpr/all_gather | solution.py:12
  134.5 47.8 %all-gather.19.cloned.1.call-done = bf16[256,96,96]{2,1,0:T(8,128)(2,1)} async-done(((bf16[16,96,96]{2,1,0:T(8,128)(2,1)}), bf16[256,96,96]{2,1,0:T(8,128)(2,1)}) %all-gather.19.cloned.1.call-update) | async-done | bytes 4718608 | tf_op jit(solution)/shard_map/while/body/eval_jaxpr/all_gather | solution.py:12
  182.3 28.5 %while.60 = (s32[]{:T(128)}, f32[16,96,96]{2,1,0:T(8,128)S(1)}, s32[]{:T(128)}, bf16[16,16]{1,0:T(8,128)(2,1)}, bf16[16,16,96,96]{3,2,1,0:T(8,128)(2,1)}, /*index=5*/s32[]{:T(128)}, s32[]{:T(128)}, s32[]{:T(128)}) while((s32[]{:T(128)}, f32[16,96,96]{2,1,0:T(8,128)S(1)}, s32[]{:T(128)}, bf16[16,16]{1,0:T(8,128)(2,1)}, ...), condition=%wide.region_8.8_spmd, body=%wide.region_7.7_spmd.sunk | while | flops 442389 | bytes 1474847 | solution.py:26
  223.8 7.9 collective-permute-done
  243.2 12.3 %all-gather.9 = bf16[16,1,16]{2,1,0:T(2,128)(2,1)S(1)} all-gather(bf16[1,1,16]{2,1,0:T(2,128)(2,1)S(1)} %fusion.82), channel_id=1, replica_groups=mesh['phase'=8,'ctx'=16,'tp'=2] {'ctx'}, dimensions={0}, use_global_device_ids=true | all-gather | bytes 544 | tf_op jit(solution)/shard_map/while/body/eval_jaxpr/all_gather | solution.py:12
  258.1 51.5 %all-gather.19.cloned.1.call-done = bf16[256,96,96]{2,1,0:T(8,128)(2,1)} async-done(((bf16[16,96,96]{2,1,0:T(8,128)(2,1)}), bf16[256,96,96]{2,1,0:T(8,128)(2,1)}) %all-gather.19.cloned.1.call-update) | async-done | bytes 4718608 | tf_op jit(solution)/shard_map/while/body/eval_jaxpr/all_gather | solution.py:12
  309.7 28.5 %while.60 = (s32[]{:T(128)}, f32[16,96,96]{2,1,0:T(8,128)S(1)}, s32[]{:T(128)}, bf16[16,16]{1,0:T(8,128)(2,1)}, bf16[16,16,96,96]{3,2,1,0:T(8,128)(2,1)}, /*index=5*/s32[]{:T(128)}, s32[]{:T(128)}, s32[]{:T(128)}) while((s32[]{:T(128)}, f32[16,96,96]{2,1,0:T(8,128)S(1)}, s32[]{:T(128)}, bf16[16,16]{1,0:T(8,128)(2,1)}, ...), condition=%wide.region_8.8_spmd, body=%wide.region_7.7_spmd.sunk | while | flops 442389 | bytes 1474847 | solution.py:26
  351.1 7.9 collective-permute-done
  370.5 12.3 %all-gather.9 = bf16[16,1,16]{2,1,0:T(2,128)(2,1)S(1)} all-gather(bf16[1,1,16]{2,1,0:T(2,128)(2,1)S(1)} %fusion.82), channel_id=1, replica_groups=mesh['phase'=8,'ctx'=16,'tp'=2] {'ctx'}, dimensions={0}, use_global_device_ids=true | all-gather | bytes 544 | tf_op jit(solution)/shard_map/while/body/eval_jaxpr/all_gather | solution.py:12
  385.4 51.5 %all-gather.19.cloned.1.call-done = bf16[256,96,96]{2,1,0:T(8,128)(2,1)} async-done(((bf16[16,96,96]{2,1,0:T(8,128)(2,1)}), bf16[256,96,96]{2,1,0:T(8,128)(2,1)}) %all-gather.19.cloned.1.call-update) | async-done | bytes 4718608 | tf_op jit(solution)/shard_map/while/body/eval_jaxpr/all_gather | solution.py:12
  437.1 28.5 %while.60 = (s32[]{:T(128)}, f32[16,96,96]{2,1,0:T(8,128)S(1)}, s32[]{:T(128)}, bf16[16,16]{1,0:T(8,128)(2,1)}, bf16[16,16,96,96]{3,2,1,0:T(8,128)(2,1)}, /*index=5*/s32[]{:T(128)}, s32[]{:T(128)}, s32[]{:T(128)}) while((s32[]{:T(128)}, f32[16,96,96]{2,1,0:T(8,128)S(1)}, s32[]{:T(128)}, bf16[16,16]{1,0:T(8,128)(2,1)}, ...), condition=%wide.region_8.8_spmd, body=%wide.region_7.7_spmd.sunk | while | flops 442389 | bytes 1474847 | solution.py:26
  478.5 7.9 collective-permute-done
  497.9 12.3 %all-gather.9 = bf16[16,1,16]{2,1,0:T(2,128)(2,1)S(1)} all-gather(bf16[1,1,16]{2,1,0:T(2,128)(2,1)S(1)} %fusion.82), channel_id=1, replica_groups=mesh['phase'=8,'ctx'=16,'tp'=2] {'ctx'}, dimensions={0}, use_global_device_ids=true | all-gather | bytes 544 | tf_op jit(solution)/shard_map/while/body/eval_jaxpr/all_gather | solution.py:12
  512.8 51.5 %all-gather.19.cloned.1.call-done = bf16[256,96,96]{2,1,0:T(8,128)(2,1)} async-done(((bf16[16,96,96]{2,1,0:T(8,128)(2,1)}), bf16[256,96,96]{2,1,0:T(8,128)(2,1)}) %all-gather.19.cloned.1.call-update) | async-done | bytes 4718608 | tf_op jit(solution)/shard_map/while/body/eval_jaxpr/all_gather | solution.py:12
  564.4 28.5 %while.60 = (s32[]{:T(128)}, f32[16,96,96]{2,1,0:T(8,128)S(1)}, s32[]{:T(128)}, bf16[16,16]{1,0:T(8,128)(2,1)}, bf16[16,16,96,96]{3,2,1,0:T(8,128)(2,1)}, /*index=5*/s32[]{:T(128)}, s32[]{:T(128)}, s32[]{:T(128)}) while((s32[]{:T(128)}, f32[16,96,96]{2,1,0:T(8,128)S(1)}, s32[]{:T(128)}, bf16[16,16]{1,0:T(8,128)(2,1)}, ...), condition=%wide.region_8.8_spmd, body=%wide.region_7.7_spmd.sunk | while | flops 442389 | bytes 1474847 | solution.py:26
  625.2 12.3 %all-gather.9 = bf16[16,1,16]{2,1,0:T(2,128)(2,1)S(1)} all-gather(bf16[1,1,16]{2,1,0:T(2,128)(2,1)S(1)} %fusion.82), channel_id=1, replica_groups=mesh['phase'=8,'ctx'=16,'tp'=2] {'ctx'}, dimensions={0}, use_global_device_ids=true | all-gather | bytes 544 | tf_op jit(solution)/shard_map/while/body/eval_jaxpr/all_gather | solution.py:12
  640.1 51.5 %all-gather.19.cloned.1.call-done = bf16[256,96,96]{2,1,0:T(8,128)(2,1)} async-done(((bf16[16,96,96]{2,1,0:T(8,128)(2,1)}), bf16[256,96,96]{2,1,0:T(8,128)(2,1)}) %all-gather.19.cloned.1.call-update) | async-done | bytes 4718608 | tf_op jit(solution)/shard_map/while/body/eval_jaxpr/all_gather | solution.py:12
  691.8 28.5 %while.60 = (s32[]{:T(128)}, f32[16,96,96]{2,1,0:T(8,128)S(1)}, s32[]{:T(128)}, bf16[16,16]{1,0:T(8,128)(2,1)}, bf16[16,16,96,96]{3,2,1,0:T(8,128)(2,1)}, /*index=5*/s32[]{:T(128)}, s32[]{:T(128)}, s32[]{:T(128)}) while((s32[]{:T(128)}, f32[16,96,96]{2,1,0:T(8,128)S(1)}, s32[]{:T(128)}, bf16[16,16]{1,0:T(8,128)(2,1)}, ...), condition=%wide.region_8.8_spmd, body=%wide.region_7.7_spmd.sunk | while | flops 442389 | bytes 1474847 | solution.py:26
  752.6 12.3 %all-gather.9 = bf16[16,1,16]{2,1,0:T(2,128)(2,1)S(1)} all-gather(bf16[1,1,16]{2,1,0:T(2,128)(2,1)S(1)} %fusion.82), channel_id=1, replica_groups=mesh['phase'=8,'ctx'=16,'tp'=2] {'ctx'}, dimensions={0}, use_global_device_ids=true | all-gather | bytes 544 | tf_op jit(solution)/shard_map/while/body/eval_jaxpr/all_gather | solution.py:12
  767.5 51.5 %all-gather.19.cloned.1.call-done = bf16[256,96,96]{2,1,0:T(8,128)(2,1)} async-done(((bf16[16,96,96]{2,1,0:T(8,128)(2,1)}), bf16[256,96,96]{2,1,0:T(8,128)(2,1)}) %all-gather.19.cloned.1.call-update) | async-done | bytes 4718608 | tf_op jit(solution)/shard_map/while/body/eval_jaxpr/all_gather | solution.py:12
  819.1 28.5 %while.60 = (s32[]{:T(128)}, f32[16,96,96]{2,1,0:T(8,128)S(1)}, s32[]{:T(128)}, bf16[16,16]{1,0:T(8,128)(2,1)}, bf16[16,16,96,96]{3,2,1,0:T(8,128)(2,1)}, /*index=5*/s32[]{:T(128)}, s32[]{:T(128)}, s32[]{:T(128)}) while((s32[]{:T(128)}, f32[16,96,96]{2,1,0:T(8,128)S(1)}, s32[]{:T(128)}, bf16[16,16]{1,0:T(8,128)(2,1)}, ...), condition=%wide.region_8.8_spmd, body=%wide.region_7.7_spmd.sunk | while | flops 442389 | bytes 1474847 | solution.py:26
  879.9 12.3 %all-gather.9 = bf16[16,1,16]{2,1,0:T(2,128)(2,1)S(1)} all-gather(bf16[1,1,16]{2,1,0:T(2,128)(2,1)S(1)} %fusion.82), channel_id=1, replica_groups=mesh['phase'=8,'ctx'=16,'tp'=2] {'ctx'}, dimensions={0}, use_global_device_ids=true | all-gather | bytes 544 | tf_op jit(solution)/shard_map/while/body/eval_jaxpr/all_gather | solution.py:12
  894.8 51.5 %all-gather.19.cloned.1.call-done = bf16[256,96,96]{2,1,0:T(8,128)(2,1)} async-done(((bf16[16,96,96]{2,1,0:T(8,128)(2,1)}), bf16[256,96,96]{2,1,0:T(8,128)(2,1)}) %all-gather.19.cloned.1.call-update) | async-done | bytes 4718608 | tf_op jit(solution)/shard_map/while/body/eval_jaxpr/all_gather | solution.py:12
  946.5 28.5 %while.60 = (s32[]{:T(128)}, f32[16,96,96]{2,1,0:T(8,128)S(1)}, s32[]{:T(128)}, bf16[16,16]{1,0:T(8,128)(2,1)}, bf16[16,16,96,96]{3,2,1,0:T(8,128)(2,1)}, /*index=5*/s32[]{:T(128)}, s32[]{:T(128)}, s32[]{:T(128)}) while((s32[]{:T(128)}, f32[16,96,96]{2,1,0:T(8,128)S(1)}, s32[]{:T(128)}, bf16[16,16]{1,0:T(8,128)(2,1)}, ...), condition=%wide.region_8.8_spmd, body=%wide.region_7.7_spmd.sunk | while | flops 442389 | bytes 1474847 | solution.py:26
  1004.8 12.3 %all-gather.4 = bf16[16,1,16]{2,1,0:T(2,128)(2,1)S(1)} all-gather(bf16[1,1,16]{2,1,0:T(2,128)(2,1)S(1)} %fusion.49), channel_id=1, replica_groups=mesh['phase'=8,'ctx'=16,'tp'=2] {'ctx'}, dimensions={0}, use_global_device_ids=true | all-gather | bytes 544 | tf_op jit(solution)/shard_map/all_gather | solution.py:12
  1019.8 51.3 %all-gather.17.cloned.1.call-done = bf16[256,96,96]{2,1,0:T(8,128)(2,1)} async-done(((bf16[16,96,96]{2,1,0:T(8,128)(2,1)}), bf16[256,96,96]{2,1,0:T(8,128)(2,1)}) %all-gather.17.cloned.1.call-update) | async-done | bytes 4718608 | tf_op jit(solution)/shard_map/all_gather | solution.py:12
  1071.2 18.7 %while.57 = (s32[]{:T(128)}, f32[16,96,96]{2,1,0:T(8,128)S(1)}, s32[]{:T(128)}, bf16[16,16]{1,0:T(8,128)(2,1)S(1)}, bf16[16,16,96,96]{3,2,1,0:T(8,128)(2,1)}, /*index=5*/s32[]{:T(128)}, s32[]{:T(128)}, s32[]{:T(128)}) while((s32[]{:T(128)}, f32[16,96,96]{2,1,0:T(8,128)S(1)}, s32[]{:T(128)}, bf16[16,16]{1,0:T(8,128)(2,1)S(1)}, ...), condition=%wide.region_16.17_spmd, body=%wide.region_15.16_spmd.sunk | while | flops 442389 | bytes 1474847 | solution.py:26
  (637 shorter events, 454.8 us)
Async XLA Ops:
  6.5 84.8 %all-gather.15.cloned.1.call-start = ((), (), s32[]{:S(2)}) async-start(), calls=%async_computation | async-start | bytes 10027008 | tf_op jit(solution)/shard_map/all_gather | solution.py:92
  8.2 42.3 %copy-start.12 = (s32[128]{0:T(128)}, s32[128]{0:T(128)S(1)}, u32[]{:S(2)}) copy-start(s32[128]{0:T(128)S(1)} %convert_reduce_fusion.1) | copy-start | bytes 1540
  9.8 41.4 %copy-start.8 = (f32[16,128]{1,0:T(8,128)}, f32[16,128]{1,0:T(8,128)S(1)}, u32[]{:S(2)}) copy-start(f32[16,128]{1,0:T(8,128)S(1)} %reduce_window_sum.28) | copy-start | bytes 24580
  20.7 26.8 %copy-start.5 = (bf16[1,16,96,288]{3,2,1,0:T(8,128)(2,1)S(1)}, bf16[1,16,96,288]{3,2,1,0:T(8,128)(2,1)}, u32[]{:S(2)}) copy-start(bf16[1,16,96,288]{3,2,1,0:T(8,128)(2,1)} %param.13) | copy-start | bytes 2654212
  106.3 76.0 %all-gather.19.cloned.1.call-start = ((), (), s32[]{:S(2)}) async-start(), calls=%async_computation.2 | async-start | bytes 6684672 | tf_op jit(solution)/shard_map/while/body/eval_jaxpr/all_gather | solution.py:12
  215.2 16.5 %copy-start.15 = (bf16[1,16]{1,0:T(2,128)(2,1)S(1)}, bf16[1,16]{1,0:T(2,128)(2,1)}, u32[]{:S(2)}) copy-start(bf16[1,16]{1,0:T(2,128)(2,1)} %copy-done.14) | copy-start | bytes 100 | tf_op jit(solution)/shard_map/while
  215.2 16.5 %copy-start.17 = (s32[4,1]{0,1:T(1,128)S(1)}, s32[4,1]{0,1:T(1,128)}, u32[]{:S(2)}) copy-start(s32[4,1]{0,1:T(1,128)} %copy-done.16) | copy-start | bytes 52 | tf_op jit(solution)/shard_map/while
  220.4 11.3 %collective-permute-start = (bf16[128,1536]{1,0:T(8,128)(2,1)S(1)}, bf16[128,1536]{1,0:T(8,128)(2,1)S(1)}, u32[]{:S(2)}, u32[]{:S(2)}) collective-permute-start(bf16[128,1536]{1,0:T(8,128)(2,1)S(1)} %fusion.84), channel_id=1, source_target_pairs={{0,32},{32,64},{64,96},{96,128},{128,160},{160,192},{192,224},{1,3... | collective-permute-start | bytes 1179656 | tf_op jit(solution)/shard_map/while/body/eval_jaxpr/ppermute | solution.py:32
  231.8 77.9 %all-gather.19.cloned.1.call-start = ((), (), s32[]{:S(2)}) async-start(), calls=%async_computation.2 | async-start | bytes 6684672 | tf_op jit(solution)/shard_map/while/body/eval_jaxpr/all_gather | solution.py:12
  342.6 16.5 %copy-start.17 = (s32[4,1]{0,1:T(1,128)S(1)}, s32[4,1]{0,1:T(1,128)}, u32[]{:S(2)}) copy-start(s32[4,1]{0,1:T(1,128)} %copy-done.16) | copy-start | bytes 52 | tf_op jit(solution)/shard_map/while
  347.8 11.3 %collective-permute-start = (bf16[128,1536]{1,0:T(8,128)(2,1)S(1)}, bf16[128,1536]{1,0:T(8,128)(2,1)S(1)}, u32[]{:S(2)}, u32[]{:S(2)}) collective-permute-start(bf16[128,1536]{1,0:T(8,128)(2,1)S(1)} %fusion.84), channel_id=1, source_target_pairs={{0,32},{32,64},{64,96},{96,128},{128,160},{160,192},{192,224},{1,3... | collective-permute-start | bytes 1179656 | tf_op jit(solution)/shard_map/while/body/eval_jaxpr/ppermute | solution.py:32
  359.1 77.9 %all-gather.19.cloned.1.call-start = ((), (), s32[]{:S(2)}) async-start(), calls=%async_computation.2 | async-start | bytes 6684672 | tf_op jit(solution)/shard_map/while/body/eval_jaxpr/all_gather | solution.py:12
  469.9 16.5 %copy-start.17 = (s32[4,1]{0,1:T(1,128)S(1)}, s32[4,1]{0,1:T(1,128)}, u32[]{:S(2)}) copy-start(s32[4,1]{0,1:T(1,128)} %copy-done.16) | copy-start | bytes 52 | tf_op jit(solution)/shard_map/while
  475.1 11.3 %collective-permute-start = (bf16[128,1536]{1,0:T(8,128)(2,1)S(1)}, bf16[128,1536]{1,0:T(8,128)(2,1)S(1)}, u32[]{:S(2)}, u32[]{:S(2)}) collective-permute-start(bf16[128,1536]{1,0:T(8,128)(2,1)S(1)} %fusion.84), channel_id=1, source_target_pairs={{0,32},{32,64},{64,96},{96,128},{128,160},{160,192},{192,224},{1,3... | collective-permute-start | bytes 1179656 | tf_op jit(solution)/shard_map/while/body/eval_jaxpr/ppermute | solution.py:32
  486.5 77.9 %all-gather.19.cloned.1.call-start = ((), (), s32[]{:S(2)}) async-start(), calls=%async_computation.2 | async-start | bytes 6684672 | tf_op jit(solution)/shard_map/while/body/eval_jaxpr/all_gather | solution.py:12
  597.3 16.5 %copy-start.15 = (bf16[1,16]{1,0:T(2,128)(2,1)S(1)}, bf16[1,16]{1,0:T(2,128)(2,1)}, u32[]{:S(2)}) copy-start(bf16[1,16]{1,0:T(2,128)(2,1)} %copy-done.14) | copy-start | bytes 100 | tf_op jit(solution)/shard_map/while
  597.3 16.5 %copy-start.17 = (s32[4,1]{0,1:T(1,128)S(1)}, s32[4,1]{0,1:T(1,128)}, u32[]{:S(2)}) copy-start(s32[4,1]{0,1:T(1,128)} %copy-done.16) | copy-start | bytes 52 | tf_op jit(solution)/shard_map/while
  602.5 11.3 %collective-permute-start = (bf16[128,1536]{1,0:T(8,128)(2,1)S(1)}, bf16[128,1536]{1,0:T(8,128)(2,1)S(1)}, u32[]{:S(2)}, u32[]{:S(2)}) collective-permute-start(bf16[128,1536]{1,0:T(8,128)(2,1)S(1)} %fusion.84), channel_id=1, source_target_pairs={{0,32},{32,64},{64,96},{96,128},{128,160},{160,192},{192,224},{1,3... | collective-permute-start | bytes 1179656 | tf_op jit(solution)/shard_map/while/body/eval_jaxpr/ppermute | solution.py:32
  613.8 77.9 %all-gather.19.cloned.1.call-start = ((), (), s32[]{:S(2)}) async-start(), calls=%async_computation.2 | async-start | bytes 6684672 | tf_op jit(solution)/shard_map/while/body/eval_jaxpr/all_gather | solution.py:12
  724.6 16.5 %copy-start.15 = (bf16[1,16]{1,0:T(2,128)(2,1)S(1)}, bf16[1,16]{1,0:T(2,128)(2,1)}, u32[]{:S(2)}) copy-start(bf16[1,16]{1,0:T(2,128)(2,1)} %copy-done.14) | copy-start | bytes 100 | tf_op jit(solution)/shard_map/while
  724.6 16.5 %copy-start.17 = (s32[4,1]{0,1:T(1,128)S(1)}, s32[4,1]{0,1:T(1,128)}, u32[]{:S(2)}) copy-start(s32[4,1]{0,1:T(1,128)} %copy-done.16) | copy-start | bytes 52 | tf_op jit(solution)/shard_map/while
  729.8 11.3 %collective-permute-start = (bf16[128,1536]{1,0:T(8,128)(2,1)S(1)}, bf16[128,1536]{1,0:T(8,128)(2,1)S(1)}, u32[]{:S(2)}, u32[]{:S(2)}) collective-permute-start(bf16[128,1536]{1,0:T(8,128)(2,1)S(1)} %fusion.84), channel_id=1, source_target_pairs={{0,32},{32,64},{64,96},{96,128},{128,160},{160,192},{192,224},{1,3... | collective-permute-start | bytes 1179656 | tf_op jit(solution)/shard_map/while/body/eval_jaxpr/ppermute | solution.py:32
  741.2 77.9 %all-gather.19.cloned.1.call-start = ((), (), s32[]{:S(2)}) async-start(), calls=%async_computation.2 | async-start | bytes 6684672 | tf_op jit(solution)/shard_map/while/body/eval_jaxpr/all_gather | solution.py:12
  852.0 16.5 %copy-start.15 = (bf16[1,16]{1,0:T(2,128)(2,1)S(1)}, bf16[1,16]{1,0:T(2,128)(2,1)}, u32[]{:S(2)}) copy-start(bf16[1,16]{1,0:T(2,128)(2,1)} %copy-done.14) | copy-start | bytes 100 | tf_op jit(solution)/shard_map/while
  852.0 16.5 %copy-start.17 = (s32[4,1]{0,1:T(1,128)S(1)}, s32[4,1]{0,1:T(1,128)}, u32[]{:S(2)}) copy-start(s32[4,1]{0,1:T(1,128)} %copy-done.16) | copy-start | bytes 52 | tf_op jit(solution)/shard_map/while
  857.2 11.3 %collective-permute-start = (bf16[128,1536]{1,0:T(8,128)(2,1)S(1)}, bf16[128,1536]{1,0:T(8,128)(2,1)S(1)}, u32[]{:S(2)}, u32[]{:S(2)}) collective-permute-start(bf16[128,1536]{1,0:T(8,128)(2,1)S(1)} %fusion.84), channel_id=1, source_target_pairs={{0,32},{32,64},{64,96},{96,128},{128,160},{160,192},{192,224},{1,3... | collective-permute-start | bytes 1179656 | tf_op jit(solution)/shard_map/while/body/eval_jaxpr/ppermute | solution.py:32
  868.5 77.9 %all-gather.19.cloned.1.call-start = ((), (), s32[]{:S(2)}) async-start(), calls=%async_computation.2 | async-start | bytes 6684672 | tf_op jit(solution)/shard_map/while/body/eval_jaxpr/all_gather | solution.py:12
  979.3 16.5 %copy-start.15 = (bf16[1,16]{1,0:T(2,128)(2,1)S(1)}, bf16[1,16]{1,0:T(2,128)(2,1)}, u32[]{:S(2)}) copy-start(bf16[1,16]{1,0:T(2,128)(2,1)} %copy-done.14) | copy-start | bytes 100 | tf_op jit(solution)/shard_map/while
  979.3 16.5 %copy-start.17 = (s32[4,1]{0,1:T(1,128)S(1)}, s32[4,1]{0,1:T(1,128)}, u32[]{:S(2)}) copy-start(s32[4,1]{0,1:T(1,128)} %copy-done.16) | copy-start | bytes 52 | tf_op jit(solution)/shard_map/while
  984.5 11.3 %collective-permute-start = (bf16[128,1536]{1,0:T(8,128)(2,1)S(1)}, bf16[128,1536]{1,0:T(8,128)(2,1)S(1)}, u32[]{:S(2)}, u32[]{:S(2)}) collective-permute-start(bf16[128,1536]{1,0:T(8,128)(2,1)S(1)} %fusion.84), channel_id=1, source_target_pairs={{0,32},{32,64},{64,96},{96,128},{128,160},{160,192},{192,224},{1,3... | collective-permute-start | bytes 1179656 | tf_op jit(solution)/shard_map/while/body/eval_jaxpr/ppermute | solution.py:32
  995.8 75.3 %all-gather.17.cloned.1.call-start = ((), (), s32[]{:S(2)}) async-start(), calls=%async_computation.1 | async-start | bytes 6684672 | tf_op jit(solution)/shard_map/all_gather | solution.py:12
  1071.2 18.7 %copy-start.10 = (f32[16,128]{1,0:T(8,128)S(1)}, f32[16,128]{1,0:T(8,128)}, u32[]{:S(2)}) copy-start(f32[16,128]{1,0:T(8,128)} %get-tuple-element.544) | copy-start | bytes 24580
  (50 other events, 530.2 us)
Sparse Core Ops, SparseCore 0:
  9.8 81.4 all-gather.14
  116.6 65.6 all-gather.18
  242.6 67.0 all-gather.18
  369.9 67.0 all-gather.18
  497.3 67.0 all-gather.18
  624.6 67.0 all-gather.18
  752.0 67.0 all-gather.18
  879.3 67.0 all-gather.18
  1004.2 66.9 all-gather.16
where the time goes:
time: 1120 us; the launch traced here: 1110 us
  waiting for transfers between devices  504 us (45%)
  other arithmetic  257 us (23%)
  blocking collectives  148 us (13%)
  matrix products  92.7 us (8%)
  local copies, waits for them, and re-layouts  53.2 us (5%)
  starting transfers between devices  22.8 us (2%)
  between operations  14.7 us (1%)
  loops' own time  14.1 us (1%)
    all_gather x8, waiting for transfers between devices, carried_in(): lax.all_gather(a.astype(kind), axis)  408 us
    add x120, other arithmetic, combine_states(): later[0][:, None, None] * earlier[1] + later[1]  143 us
    all_gather x8, blocking collectives, carried_in(): lax.all_gather(a.astype(kind), axis)  101 us
    convert_element_type x120, other arithmetic, one(): lax.dynamic_index_in_dim(a, lap, 0, False).astype(own.dtype)  71.4 us
    ppermute x7, waiting for transfers between devices, from_behind(): return lax.ppermute(block, axis, route)  55.5 us
    dot_general x8, matrix products, add_heads(): return jnp.dot(piece, out_weight, preferred_element_type=jnp.float32)  42.2 us
    all_gather x1, waiting for transfers between devices, shards(): mantissa_all = lax.all_gather(out_mantissa[0], 'ctx', axis=0, tiled=True)  39.5 us
    mul x2, local copies, waits for them, and re-layouts, dequantize(): blocks * scale[:, None, :, None]  36.7 us
  transfers between devices with their start and end apart: 16, of which 16 were waited for; matrix products, arithmetic and copies ran while one was open for 6% of the time, Pallas kernels for 0%

commit v1 on v0

v1 whole, which is shorter than its diff:
```python
import jax
import jax.numpy as jnp
from jax import lax
from jax.experimental import pallas as pl
from jax.experimental.pallas import tpu as pltpu
from jax.sharding import PartitionSpec as P

EPSILON = 1e-05
MESH = pl.DeviceIdType.MESH
LAYERS = 8
BLOCKS = 16
ROWS = 128
HEAD = 96
OWN = 4
WIDE = OWN * HEAD
MODEL = 3072
F32 = jnp.float32
BF16 = jnp.bfloat16


def contract(a, b, da, db):
    return lax.dot_general(a, b, (((da,), (db,)), ((), ())), preferred_element_type=F32)


def kernel(
    hid, wd, qk, ld, lens, out,
    xbuf, sbuf, nbuf, tbuf, wbuf, qbuf, graw, gbuf, cbuf, mbuf, wst, qst, wsrc, qsrc,
    bits, ldsend, hsem, sibsend, sibsem, gsem, csend, csem,
    ssend, ssem, tsend, tsem, nsend, nsem, osend, osem,
    zsend, zsem, rsend, wsem, qsem,
):
    z, c, t = lax.axis_index("phase"), lax.axis_index("ctx"), lax.axis_index("tp")
    y = lax.rem(c, 4)
    zq, zr = z // 4, lax.rem(z, 4)

    def push(src, dst, s, r, dev):
        return pltpu.make_async_remote_copy(
            src_ref=src, dst_ref=dst, send_sem=s, recv_sem=r, device_id=dev, device_id_type=MESH
        )

    def arrived(dst, r):
        push(dst, dst, r, r, (z, c, 1 - t)).wait_recv()

    def sent(src, s):
        push(src, src, s, s, (z, c, 1 - t)).wait_send()

    def cols(ref, k):
        return ref.at[:, pl.ds(pl.multiple_of(WIDE * k, 128), WIDE)]

    barrier = pltpu.get_barrier_semaphore()

    def greet(dev):
        pl.semaphore_signal(barrier, inc=1, device_id=dev, device_id_type=MESH)

    greet((z, c, 1 - t))
    for d in range(1, LAYERS):
        for core in range(2):
            greet((lax.rem(z + d, LAYERS), c, core))

    def greet_plane(d, carry):
        there = lax.rem(c + d, BLOCKS)
        greet((z, there, 1))

        @pl.when(t == 1)
        def _():
            greet((z, there, 0))

        return carry

    lax.fori_loop(1, BLOCKS, greet_plane, 0)

    @pl.when(t == 1)
    def _():
        pl.semaphore_wait(barrier, 45)

    @pl.when(t == 0)
    def _():
        pl.semaphore_wait(barrier, 30)

    hid_local = pltpu.make_async_copy(cols(hid, zr), xbuf, hsem)
    hid_remote = push(cols(hid, zr), xbuf, sibsend.at[6], hsem, (z, c, 1))

    @pl.when((t == 1) & (zq == 1))
    def _():
        hid_local.start()

    @pl.when((t == 0) & (zq == 0))
    def _():
        hid_remote.start()

    for k in range(4):
        mine = (t == 1) & (zq == 1) & (zr == k)

        @pl.when(mine)
        def _():
            pltpu.make_async_copy(ld.at[k], graw.at[z], gsem.at[z]).start()

        @pl.when(jnp.logical_not(mine))
        def _():
            push(ld.at[k], graw.at[z], ldsend.at[k], gsem.at[z], (4 * t + k, c, 1)).start()

    @pl.when(t == 0)
    def _():
        distribute(z, c, y, zq, zr, push, arrived, sent, cols, wd, qk, wst, qst, wsrc, qsrc, wbuf, qbuf,
                   sibsem, zsend, zsem, rsend, wsem, qsem)

    @pl.when(t == 1)
    def _():
        for k in range(4):
            push(qk.at[4 * k + y], qsrc.at[k], sibsend.at[k], sibsem.at[k], (z, c, 0)).start()
        push(wd, wsrc, sibsend.at[4], sibsem.at[4], (z, c, 0)).start()
        layers(z, c, zq, zr, push, arrived, sent, cols, hid_local, hid_remote, lens, out,
               xbuf, sbuf, nbuf, tbuf, wbuf, qbuf, graw, gbuf, cbuf, mbuf, bits,
               gsem, csend, csem, ssend, ssem, tsend, tsem, nsend, nsem, osend, osem, wsem, qsem)
        for k in range(4):
            sent(qsrc.at[k], sibsend.at[k])
        sent(wsrc, sibsend.at[4])

    @pl.when((t == 0) & (zq == 0))
    def _():
        hid_remote.wait_send()

    for k in range(4):
        mine = (t == 1) & (zq == 1) & (zr == k)

        @pl.when(jnp.logical_not(mine))
        def _():
            sent(ld.at[k], ldsend.at[k])
            arrived(cols(out, k), osem.at[k])


def distribute(z, c, y, zq, zr, push, arrived, sent, cols, wd, qk, wst, qst, wsrc, qsrc, wbuf, qbuf,
               sibsem, zsend, zsem, rsend, wsem, qsem):
    base = c - y
    for k in range(4):
        arrived(qsrc.at[k], sibsem.at[k])
    arrived(wsrc, sibsem.at[4])

    def step(l, carry):
        @pl.when(z == l)
        def _():
            for kind in range(2):
                for d in (4, 3, 5, 2, 6, 1, 7, 0):
                    there = lax.rem(z + d, LAYERS)
                    k = lax.rem(there, 4)
                    for half in range(2):

                        @pl.when(there // 4 == half)
                        def _():
                            if kind == 0:
                                src = qsrc.at[k] if half else qk.at[4 * k + y]
                                dst = qst.at[l]
                            else:
                                src = cols(wsrc if half else wd, k)
                                dst = wst.at[l]
                            if d:
                                push(src, dst, zsend.at[kind, d], zsem.at[kind, l], (there, c, 0)).start()
                            else:
                                pltpu.make_async_copy(src, dst, zsem.at[kind, l]).start()

        @pl.when(z == l)
        def _():
            pltpu.make_async_copy(qst.at[l], qst.at[l], zsem.at[0, l]).wait()

        @pl.when(z != l)
        def _():
            arrived(qst.at[l], zsem.at[0, l])

        for yy in range(4):
            push(qst.at[l], qbuf.at[l, y], rsend.at[16 + yy], qsem.at[l, y], (z, base + yy, 1)).start()

        @pl.when(z == l)
        def _():
            pltpu.make_async_copy(wst.at[l], wst.at[l], zsem.at[1, l]).wait()

        @pl.when(z != l)
        def _():
            arrived(wst.at[l], zsem.at[1, l])

        def relay(d, carry):
            there = lax.rem(c + d, BLOCKS)
            push(wst.at[l], wbuf.at[l, c], rsend.at[d], wsem.at[l, c], (z, there, 1)).start()
            return carry

        lax.fori_loop(0, BLOCKS, relay, 0)
        for yy in range(4):
            sent(qst.at[l], rsend.at[16 + yy])

        def relayed(d, carry):
            sent(wst.at[l], rsend.at[d])
            return carry

        lax.fori_loop(0, BLOCKS, relayed, 0)

        @pl.when(z == l)
        def _():
            for d in range(1, LAYERS):
                sent(qst.at[l], zsend.at[0, d])
                sent(wst.at[l], zsend.at[1, d])

        return carry

    lax.fori_loop(0, LAYERS, step, 0)


def layers(z, c, zq, zr, push, arrived, sent, cols, hid_local, hid_remote, lens, out,
           xbuf, sbuf, nbuf, tbuf, wbuf, qbuf, graw, gbuf, cbuf, mbuf, bits,
           gsem, csend, csem, ssend, ssem, tsend, tsem, nsend, nsem, osend, osem, wsem, qsem):
    e1 = lens[0, 0]
    e2 = e1 + lens[0, 1]
    e3 = e2 + lens[0, 2]

    def segment(p):
        return (p >= e1).astype(jnp.int32) + (p >= e2).astype(jnp.int32) + (p >= e3).astype(jnp.int32)

    first = c * ROWS
    seg_row = segment(first + lax.broadcasted_iota(jnp.int32, (ROWS, ROWS), 1))
    seg_col = segment(first + lax.broadcasted_iota(jnp.int32, (ROWS, ROWS), 0))
    later = lax.broadcasted_iota(jnp.int32, (ROWS, ROWS), 0) <= lax.broadcasted_iota(jnp.int32, (ROWS, ROWS), 1)
    small = first + lax.broadcasted_iota(jnp.int32, (8, ROWS), 1)
    seg_small = segment(small)
    seg_last = segment(jnp.full((8, ROWS), first + ROWS - 1, jnp.int32))
    before = jnp.where(c == 0, jnp.full((8, ROWS), -1, jnp.int32), segment(jnp.full((8, ROWS), first - 1, jnp.int32)))
    bits[0] = (seg_small == seg_last).astype(F32)
    bits[1] = (seg_small == before).astype(F32)
    bits[2] = (seg_last == before).astype(F32)
    lane8 = lax.broadcasted_iota(jnp.int32, (8, ROWS), 1)

    for l in range(LAYERS):
        mine = (zq == 1) & (z == l)

        @pl.when(mine)
        def _():
            pltpu.make_async_copy(graw.at[l], graw.at[l], gsem.at[l]).wait()

        @pl.when(jnp.logical_not(mine))
        def _():
            arrived(graw.at[l], gsem.at[l])

    def decays(l, carry):
        g = graw[l]
        for s in (1, 2, 4, 8, 16, 32, 64):
            g = g + jnp.where(lane8 >= s, pltpu.roll(g, s, 1), 0.0)
        gbuf[l] = g
        kept = jnp.exp(jnp.broadcast_to(g[:, ROWS - 1 :], (8, ROWS))) * bits[2]
        cbuf[c, l] = jnp.where(lane8 < HEAD, kept, jnp.broadcast_to(kept[3:4], (8, ROWS)))
        return carry

    lax.fori_loop(0, LAYERS, decays, 0)

    def tell(there, carry):
        push(cbuf.at[c], cbuf.at[c], csend.at[there], csem.at[c], (z, there, 1)).start()
        return carry

    lax.fori_loop(c + 1, BLOCKS, tell, 0)
    allowed = later & (seg_row == seg_col)

    def masks(l, carry):
        for h in range(OWN):
            row = jnp.broadcast_to(gbuf[l, h : h + 1], (ROWS, ROWS))
            mbuf[l, h] = jnp.exp(jnp.where(allowed, row - row.T, -1e30))
        return carry

    lax.fori_loop(0, LAYERS, masks, 0)

    @pl.when(zq == 1)
    def _():
        hid_local.wait()

    @pl.when(zq == 0)
    def _():
        hid_remote.wait_recv()

    def heard(there, carry):
        arrived(cbuf.at[there], csem.at[there])
        return carry

    lax.fori_loop(0, c, heard, 0)
    lane96 = lax.broadcasted_iota(jnp.int32, (HEAD, ROWS), 1)

    def emit(l):
        self_kept = (zq == 1) & (z == l)

        @pl.when(self_kept)
        def _():
            pltpu.make_async_copy(xbuf, cols(out, zr), osem.at[zr]).start()

        @pl.when(jnp.logical_not(self_kept))
        def _():
            push(xbuf, cols(out, zr), osend, osem.at[zr], (l, c, zq)).start()

    def emitted(l):
        self_kept = (zq == 1) & (z == l)

        @pl.when(self_kept)
        def _():
            pltpu.make_async_copy(xbuf, cols(out, zr), osem.at[zr]).wait()

        @pl.when(jnp.logical_not(self_kept))
        def _():
            sent(xbuf, osend)

    def layer(l, carry):
        x = xbuf[...]
        xt = x.astype(F32).T
        own_squares = jnp.sum(xt * xt, axis=0, keepdims=True)
        sbuf[l, z] = own_squares
        for d in (4, 3, 5, 2, 6, 1, 7):
            push(sbuf.at[l, z], sbuf.at[l, z], ssend.at[d], ssem.at[l, z], (lax.rem(z + d, LAYERS), c, 1)).start()
        for h in range(OWN):
            arrived(qbuf.at[l, h], qsem.at[l, h])
        squares = own_squares
        for d in (1, 7, 2, 6, 3, 5, 4):
            there = lax.rem(z + d, LAYERS)
            arrived(sbuf.at[l, there], ssem.at[l, there])
            squares = squares + sbuf[l, there]
        xtb = (xt * lax.rsqrt(squares / MODEL + EPSILON)).astype(BF16)
        raw = [contract(qbuf[l, h], xtb[HEAD * h : HEAD * h + HEAD], 1, 0) for h in range(OWN)]

        @pl.when(l > 0)
        def _():
            emit(l - 1)

        g = gbuf[l]
        key_scale = jnp.exp(jnp.broadcast_to(g[:, ROWS - 1 :], (8, ROWS)) - g) * bits[0]
        query_scale = jnp.exp(g) * bits[1]
        keys, values, keyed = [], [], []
        for h in range(OWN):
            k = jax.nn.silu(raw[h][HEAD : 2 * HEAD]).astype(BF16)
            keys.append(k)
            values.append(raw[h][2 * HEAD :].astype(BF16))
            keyed.append((k.astype(F32) * key_scale[h : h + 1]).astype(BF16))
        for p in range(3):
            right = jnp.concatenate([keyed[p], keyed[3][32 * p : 32 * p + 32]], axis=0)
            both = contract(jnp.concatenate([values[p], values[3]], axis=0), right, 1, 1)
            tbuf[l, c, HEAD * p : HEAD * p + HEAD] = jnp.where(lane96 < HEAD, both[:HEAD], both[HEAD:]).astype(BF16)

        def states_out(there, carry):
            push(tbuf.at[l, c], tbuf.at[l, c], tsend.at[there], tsem.at[l, c], (z, there, 1)).start()
            return carry

        lax.fori_loop(c + 1, BLOCKS, states_out, 0)

        inner, queried = [], []
        for h in range(OWN):
            q = jax.nn.silu(raw[h][:HEAD]).astype(BF16)
            scores = contract(keys[h], q, 0, 0)
            weights = (scores * mbuf[l, h]).astype(BF16)
            inner.append(contract(values[h], weights, 1, 0))
            queried.append((q.astype(F32) * query_scale[h : h + 1]).astype(BF16))

        def fold(there, state):
            arrived(tbuf.at[l, there], tsem.at[l, there])
            return tuple(
                s * cbuf[there, l, p : p + 1] + tbuf[l, there, HEAD * p : HEAD * p + HEAD].astype(F32)
                for p, s in enumerate(state)
            )

        state = lax.fori_loop(0, c, fold, tuple(jnp.zeros((HEAD, ROWS), F32) for _ in range(3)))
        attended = list(inner)
        for p in range(3):
            left = jnp.concatenate([queried[p], jnp.zeros((32, ROWS), BF16)], axis=0)
            right = jnp.concatenate([jnp.zeros((HEAD, ROWS), BF16), queried[3][32 * p : 32 * p + 32]], axis=0)
            both = contract(state[p].astype(BF16), jnp.concatenate([left, right], axis=1), 1, 0)
            attended[p] = attended[p] + both[:, :ROWS]
            attended[3] = attended[3] + both[:, ROWS:]
        normed = [a * lax.rsqrt(jnp.mean(a * a, axis=0, keepdims=True) + EPSILON) for a in attended]
        nbuf[l, z] = jnp.concatenate(normed, axis=0).T.astype(BF16)
        for d in (4, 3, 5, 2, 6, 1, 7):
            push(nbuf.at[l, z], nbuf.at[l, z], nsend.at[d], nsem.at[l, z], (lax.rem(z + d, LAYERS), c, 1)).start()

        total = x.astype(F32)
        for d in (0, 1, 7, 2, 6, 3, 5, 4):
            there = lax.rem(z + d, LAYERS)
            for half in range(2):
                arrived(wbuf.at[l, 2 * there + half], wsem.at[l, 2 * there + half])
            if d:
                arrived(nbuf.at[l, there], nsem.at[l, there])
            weight = wbuf[l, pl.ds(2 * there, 2)].reshape(WIDE, WIDE)
            total = total + contract(nbuf[l, there], weight, 1, 0)

        @pl.when(l > 0)
        def _():
            emitted(l - 1)

        xbuf[...] = total.astype(BF16)
        for d in range(1, LAYERS):
            sent(sbuf.at[l, z], ssend.at[d])
            sent(nbuf.at[l, z], nsend.at[d])

        def states_sent(there, carry):
            sent(tbuf.at[l, c], tsend.at[there])
            return carry

        lax.fori_loop(c + 1, BLOCKS, states_sent, 0)
        return carry

    lax.fori_loop(0, LAYERS, layer, 0)
    emit(LAYERS - 1)
    emitted(LAYERS - 1)

    def told(there, carry):
        sent(cbuf.at[c], csend.at[there])
        return carry

    lax.fori_loop(c + 1, BLOCKS, told, 0)


def shards(hidden_in, qkv_weight, log_decay, lengths, out_mantissa, out_exponent):
    ctx = lax.axis_index("ctx")
    exponent = lax.dynamic_slice_in_dim(out_exponent[0], 2 * ctx, 2, 0)
    scale = jnp.exp2(exponent.astype(F32))
    scale = jnp.repeat(scale, HEAD, axis=1)[:, None, :]
    weight = (out_mantissa[0].astype(F32).reshape(2, HEAD, -1) * scale).reshape(2 * HEAD, -1).astype(BF16)
    qkv = qkv_weight[0].swapaxes(1, 2)
    decay = jnp.pad(log_decay[0, 0].T.reshape(4, OWN, ROWS), ((0, 0), (0, 8 - OWN), (0, 0)))
    half = hidden_in.shape[2]
    dma = pltpu.SemaphoreType.DMA
    anywhere = pl.BlockSpec(memory_space=pl.ANY)
    outputs = pl.pallas_call(
        kernel,
        out_shape=jax.ShapeDtypeStruct((ROWS, half), BF16),
        in_specs=[anywhere] * 4 + [pl.BlockSpec(memory_space=pltpu.SMEM)],
        out_specs=anywhere,
        scratch_shapes=[
            pltpu.VMEM((ROWS, WIDE), BF16),
            pltpu.VMEM((LAYERS, LAYERS, 1, ROWS), F32),
            pltpu.VMEM((LAYERS, LAYERS, ROWS, WIDE), BF16),
            pltpu.VMEM((LAYERS, BLOCKS, 3 * HEAD, ROWS), BF16),
            pltpu.VMEM((LAYERS, BLOCKS, 2 * HEAD, WIDE), BF16),
            pltpu.VMEM((LAYERS, OWN, 3 * HEAD, HEAD), BF16),
            pltpu.VMEM((LAYERS, 8, ROWS), F32),
            pltpu.VMEM((LAYERS, 8, ROWS), F32),
            pltpu.VMEM((BLOCKS, LAYERS, 8, ROWS), F32),
            pltpu.VMEM((LAYERS, OWN, ROWS, ROWS), F32),
            pltpu.VMEM((LAYERS, 2 * HEAD, WIDE), BF16),
            pltpu.VMEM((LAYERS, 3 * HEAD, HEAD), BF16),
            pltpu.VMEM((2 * HEAD, half), BF16),
            pltpu.VMEM((4, 3 * HEAD, HEAD), BF16),
            pltpu.VMEM((3, 8, ROWS), F32),
            dma((4,)),
            dma,
            dma((7,)),
            dma((5,)),
            dma((LAYERS,)),
            dma((BLOCKS,)),
            dma((BLOCKS,)),
            dma((LAYERS,)),
            dma((LAYERS, LAYERS)),
            dma((BLOCKS,)),
            dma((LAYERS, BLOCKS)),
            dma((LAYERS,)),
            dma((LAYERS, LAYERS)),
            dma,
            dma((4,)),
            dma((2, LAYERS)),
            dma((2, LAYERS)),
            dma((20,)),
            dma((LAYERS, BLOCKS)),
            dma((LAYERS, OWN)),
        ],
        compiler_params=pltpu.CompilerParams(collective_id=0, has_side_effects=True, vmem_limit_bytes=58 << 20),
    )(hidden_in[0], weight, qkv, decay, lengths)
    return outputs[None, None]


def solution(mesh):
    in_specs = (
        P(None, "ctx", "tp"),
        P("phase", "tp", None, None),
        P("phase", None, "ctx", "tp"),
        P(),
        P("phase", "ctx", "tp"),
        P("phase", None, "tp"),
    )
    out_specs = P("phase", None, "ctx", "tp")
    return jax.shard_map(shards, mesh=mesh, in_specs=in_specs, out_specs=out_specs, check_vma=False)
```

time: 1120 us -> 310 us (0.28); the launches traced: 1110 us -> 309 us
  waiting for transfers between devices: 504 us -> 0 us
  Pallas kernels: 0 us -> 302 us
  other arithmetic: 257 us -> 2.87 us
  blocking collectives: 148 us -> 0 us
  matrix products: 92.7 us -> 0 us
  local copies, waits for them, and re-layouts: 53.2 us -> 4.82 us
  starting transfers between devices: 22.8 us -> 0 us
  between operations: 14.7 us -> 0.02 us
  loops' own time: 14.1 us -> 0 us
    all_gather x9 -> x0, waiting for transfers between devices: 448 us -> none  [the longest x8 408 us: carried_in(): lax.all_gather(a.astype(kind), axis)]
    pallas_call x0 -> x1, Pallas kernels: none -> 302 us  [shards(): pl.pallas_call(kernel, out_shape=jax.ShapeDtypeStruct((ROWS, half), BF16)...]
    add x128 -> x0, other arithmetic: 143 us -> none  [the longest x120 143 us: combine_states(): later[0][:, None, None] * earlier[1] + later[1]]
    all_gather x16 -> x0, blocking collectives: 122 us -> none  [the longest x8 101 us: carried_in(): lax.all_gather(a.astype(kind), axis)]
    dot_general x40 -> x0, matrix products: 92.7 us -> none  [the longest x8 42.2 us: add_heads(): return jnp.dot(piece, out_weight, preferred_element_type=jnp.float32)]
    convert_element_type x145 -> x1, other arithmetic: 92.3 us -> 2 us  [shards(): (out_mantissa[0].astype(F32).reshape(2, HEAD, -1) * scale).reshape(2 * HE...]
    ppermute x7 -> x0, waiting for transfers between devices: 55.5 us -> none  [from_behind(): return lax.ppermute(block, axis, route)]
    mul x9 -> x1, local copies, waits for them, and re-layouts: 37.1 us -> 0.09 us  [shards(): out_mantissa[0].astype(F32).reshape(2, HEAD, -1) * scale]
  transfers between devices with their start and end apart: 16 -> 0, of which waited for: 16 -> 0; matrix products, arithmetic and copies ran while one was open for 6% -> 0% of each run, Pallas kernels for 0% -> 0%
where the time goes in v1:
time: 310 us; the launch traced here: 309 us
  Pallas kernels  302 us (97%)
  local copies, waits for them, and re-layouts  4.82 us (2%)
    pallas_call x1, Pallas kernels, shards(): pl.pallas_call(kernel, out_shape=jax.ShapeDtypeStruct((ROWS, half), BF16)...  302 us

profile of v1, /device:TPU:31, one launch (start us, length us, event | category | flops | bytes accessed | tf_op | source)
XLA Modules:
  0.0 309.3 jit_solution(15388056946898586059)
XLA Ops:
  0.0 0.0 copy-start
  0.0 0.9 multiply_exponential_fusion
  0.9 0.1 copy.12
  1.0 0.1 broadcast_in_dim.6
  1.0 0.1 mul.13
  1.1 1.3 pad.4.ld
  2.4 2.0 fusion.wd
  4.4 0.0 copy-done
  4.4 1.5 copy.10
  5.9 301.6 %shard_map.64 = bf16[128,1536]{1,0:T(8,128)(2,1)} custom-call(bf16[128,1536]{1,0:T(8,128)(2,1)} %bitcast.18, bf16[192,1536]{1,0:T(8,128)(2,1)} %fusion.wd, bf16[16,288,96]{2,1,0:T(8,128)(2,1)} %bitcast.16, f32[4,8,128]{2,1,0:T(8,128)} %pad.4.ld, s32[1,4]{1,0:T(1,128)} %lens.1), custom_call_target="tpu_custom_call" | custom-call | tf_op jit(solution)/shard_map/pallas_call | solution.py:420
  307.5 1.8 copy.14
Async XLA Ops:
  0.0 4.4 %copy-start = (bf16[1,16,96,288]{3,2,1,0:T(8,128)(2,1)S(1)}, bf16[1,16,96,288]{3,2,1,0:T(8,128)(2,1)}, u32[]{:S(2)}) copy-start(bf16[1,16,96,288]{3,2,1,0:T(8,128)(2,1)} %param.7) | copy-start | bytes 2654212

commit v2 on v1

--- a/solution.py
+++ b/solution.py
@@ -27,7 +27,7 @@
     xbuf, sbuf, nbuf, tbuf, wbuf, qbuf, graw, gbuf, cbuf, mbuf, wst, qst, wsrc, qsrc,
     bits, ldsend, hsem, sibsend, sibsem, gsem, csend, csem,
     ssend, ssem, tsend, tsem, nsend, nsem, osend, osem,
-    zsend, zsem, rsend, wsem, qsem,
+    zsend, zsem, psend, psem, rsend, wsem, qsem,
 ):
     z, c, t = lax.axis_index("phase"), lax.axis_index("ctx"), lax.axis_index("tp")
     y = lax.rem(c, 4)
@@ -58,24 +58,12 @@
             greet((lax.rem(z + d, LAYERS), c, core))
 
     def greet_plane(d, carry):
-        there = lax.rem(c + d, BLOCKS)
-        greet((z, there, 1))
-
-        @pl.when(t == 1)
-        def _():
-            greet((z, there, 0))
-
+        for core in range(2):
+            greet((z, lax.rem(c + d, BLOCKS), core))
         return carry
 
     lax.fori_loop(1, BLOCKS, greet_plane, 0)
-
-    @pl.when(t == 1)
-    def _():
-        pl.semaphore_wait(barrier, 45)
-
-    @pl.when(t == 0)
-    def _():
-        pl.semaphore_wait(barrier, 30)
+    pl.semaphore_wait(barrier, 2 * (LAYERS + BLOCKS) - 3)
 
     hid_local = pltpu.make_async_copy(cols(hid, zr), xbuf, hsem)
     hid_remote = push(cols(hid, zr), xbuf, sibsend.at[6], hsem, (z, c, 1))
@@ -102,7 +90,7 @@
     @pl.when(t == 0)
     def _():
         distribute(z, c, y, zq, zr, push, arrived, sent, cols, wd, qk, wst, qst, wsrc, qsrc, wbuf, qbuf,
-                   sibsem, zsend, zsem, rsend, wsem, qsem)
+                   sibsem, zsend, zsem, psend, psem, rsend, wsem, qsem)
 
     @pl.when(t == 1)
     def _():
@@ -130,77 +118,100 @@
 
 
 def distribute(z, c, y, zq, zr, push, arrived, sent, cols, wd, qk, wst, qst, wsrc, qsrc, wbuf, qbuf,
-               sibsem, zsend, zsem, rsend, wsem, qsem):
-    base = c - y
-    for k in range(4):
-        arrived(qsrc.at[k], sibsem.at[k])
-    arrived(wsrc, sibsem.at[4])
+               sibsem, zsend, zsem, psend, psem, rsend, wsem, qsem):
+    x4 = c - y
+    upper, lower = pl.ds(0, HEAD), pl.ds(HEAD, HEAD)
+
+    def scatter():
+        for kind in range(2):
+            for half in range(2):
+                if half and kind == 0:
+                    for k in range(4):
+                        arrived(qsrc.at[k], sibsem.at[k])
+                if half and kind == 1:
+                    arrived(wsrc, sibsem.at[4])
+                for k in range(4):
+                    there = 4 * half + k
+                    if kind == 0:
+                        src = qsrc.at[k] if half else qk.at[4 * k + y]
+                        dst = qst.at[z]
+                    else:
+                        src = cols(wsrc if half else wd, k)
+                        dst = wst.at[z]
+
+                    @pl.when(z != there)
+                    def _():
+                        push(src, dst, zsend.at[kind, there], zsem.at[kind, z], (there, c, 0)).start()
+
+                    @pl.when(z == there)
+                    def _():
+                        pltpu.make_async_copy(src, dst, zsem.at[kind, z]).start()
+
+    def staged(kind, l, ref):
+        @pl.when(z == l)
+        def _():
+            pltpu.make_async_copy(ref.at[l], ref.at[l], zsem.at[kind, l]).wait()
+
+        @pl.when(z != l)
+        def _():
+            arrived(ref.at[l], zsem.at[kind, l])
+
+    @pl.when(z == 0)
+    def _():
+        scatter()
 
     def step(l, carry):
-        @pl.when(z == l)
-        def _():
-            for kind in range(2):
-                for d in (4, 3, 5, 2, 6, 1, 7, 0):
-                    there = lax.rem(z + d, LAYERS)
-                    k = lax.rem(there, 4)
-                    for half in range(2):
-
-                        @pl.when(there // 4 == half)
-                        def _():
-                            if kind == 0:
-                                src = qsrc.at[k] if half else qk.at[4 * k + y]
-                                dst = qst.at[l]
-                            else:
-                                src = cols(wsrc if half else wd, k)
-                                dst = wst.at[l]
-                            if d:
-                                push(src, dst, zsend.at[kind, d], zsem.at[kind, l], (there, c, 0)).start()
-                            else:
-                                pltpu.make_async_copy(src, dst, zsem.at[kind, l]).start()
-
-        @pl.when(z == l)
-        def _():
-            pltpu.make_async_copy(qst.at[l], qst.at[l], zsem.at[0, l]).wait()
-
-        @pl.when(z != l)
-        def _():
-            arrived(qst.at[l], zsem.at[0, l])
-
+        staged(0, l, qst)
         for yy in range(4):
-            push(qst.at[l], qbuf.at[l, y], rsend.at[16 + yy], qsem.at[l, y], (z, base + yy, 1)).start()
-
-        @pl.when(z == l)
-        def _():
-            pltpu.make_async_copy(wst.at[l], wst.at[l], zsem.at[1, l]).wait()
-
-        @pl.when(z != l)
-        def _():
-            arrived(wst.at[l], zsem.at[1, l])
-
-        def relay(d, carry):
-            there = lax.rem(c + d, BLOCKS)
-            push(wst.at[l], wbuf.at[l, c], rsend.at[d], wsem.at[l, c], (z, there, 1)).start()
-            return carry
-
-        lax.fori_loop(0, BLOCKS, relay, 0)
-        for yy in range(4):
-            sent(qst.at[l], rsend.at[16 + yy])
-
-        def relayed(d, carry):
-            sent(wst.at[l], rsend.at[d])
-            return carry
-
-        lax.fori_loop(0, BLOCKS, relayed, 0)
-
-        @pl.when(z == l)
-        def _():
-            for d in range(1, LAYERS):
-                sent(qst.at[l], zsend.at[0, d])
-                sent(wst.at[l], zsend.at[1, d])
-
+            push(qst.at[l], qbuf.at[l, y], rsend.at[l, 32 + yy], qsem.at[l], (z, x4 + yy, 1)).start()
+        staged(1, l, wst)
+        for d in range(1, 4):
+            push(wst.at[l, upper], wbuf.at[l, c, upper], psend.at[l, 0, d], psem.at[l, 0, c // 4],
+                 (z, lax.rem(c + 4 * d, BLOCKS), 0)).start()
+            push(wst.at[l, lower], wbuf.at[l, c, lower], psend.at[l, 1, d], psem.at[l, 1, y],
+                 (z, x4 + lax.rem(y + d, 4), 0)).start()
+
+        @pl.when((l == 0) & (z > 0))
+        def _():
+            scatter()
+
+        for d in range(4):
+            across = lax.rem(c + 4 * d, BLOCKS)
+            along = x4 + lax.rem(y + d, 4)
+            if d:
+                arrived(wbuf.at[l, across, upper], psem.at[l, 0, across // 4])
+                arrived(wbuf.at[l, along, lower], psem.at[l, 1, along - x4])
+            for e in (1, 3, 2, 0):
+                src = wbuf.at[l, across, upper] if d else wst.at[l, upper]
+                push(src, wbuf.at[l, across, upper], rsend.at[l, 4 * d + e], wsem.at[l],
+                     (z, x4 + lax.rem(y + e, 4), 1)).start()
+                src = wbuf.at[l, along, lower] if d else wst.at[l, lower]
+                push(src, wbuf.at[l, along, lower], rsend.at[l, 16 + 4 * d + e], wsem.at[l],
+                     (z, lax.rem(c + 4 * e, BLOCKS), 1)).start()
         return carry
 
     lax.fori_loop(0, LAYERS, step, 0)
+    for there in range(LAYERS):
+
+        @pl.when(z != there)
+        def _():
+            sent(qst.at[z], zsend.at[0, there])
+            sent(wst.at[z], zsend.at[1, there])
+
+    def finish(l, carry):
+        for e in range(4):
+            sent(qst.at[l], rsend.at[l, 32 + e])
+            for d in range(1, 4):
+                if e < 2:
+                    sent(wst.at[l, upper], psend.at[l, e, d])
+
+        def one(e, inner):
+            sent(wst.at[l, upper], rsend.at[l, e])
+            return inner
+
+        return lax.fori_loop(0, 32, one, carry)
+
+    lax.fori_loop(0, LAYERS, finish, 0)
 
 
 def layers(z, c, zq, zr, push, arrived, sent, cols, hid_local, hid_remote, lens, out,
@@ -307,8 +318,7 @@
         sbuf[l, z] = own_squares
         for d in (4, 3, 5, 2, 6, 1, 7):
             push(sbuf.at[l, z], sbuf.at[l, z], ssend.at[d], ssem.at[l, z], (lax.rem(z + d, LAYERS), c, 1)).start()
-        for h in range(OWN):
-            arrived(qbuf.at[l, h], qsem.at[l, h])
+        arrived(qbuf.at[l], qsem.at[l])
         squares = own_squares
         for d in (1, 7, 2, 6, 3, 5, 4):
             there = lax.rem(z + d, LAYERS)
@@ -366,18 +376,37 @@
             attended[3] = attended[3] + both[:, ROWS:]
         normed = [a * lax.rsqrt(jnp.mean(a * a, axis=0, keepdims=True) + EPSILON) for a in attended]
         nbuf[l, z] = jnp.concatenate(normed, axis=0).T.astype(BF16)
-        for d in (4, 3, 5, 2, 6, 1, 7):
-            push(nbuf.at[l, z], nbuf.at[l, z], nsend.at[d], nsem.at[l, z], (lax.rem(z + d, LAYERS), c, 1)).start()
-
-        total = x.astype(F32)
-        for d in (0, 1, 7, 2, 6, 3, 5, 4):
+        def onward(source, rows, slot, d):
+            part = nbuf.at[l, source, rows]
+            return push(part, part, nsend.at[slot], nsem.at[l, source], (lax.rem(z + d, LAYERS), c, 1))
+
+        every, early, late = pl.ds(0, ROWS), pl.ds(0, ROWS // 2), pl.ds(ROWS // 2, ROWS // 2)
+        behind, ahead = lax.rem(z + 6, LAYERS), lax.rem(z + 2, LAYERS)
+        copies = [onward(z, every, slot, d) for slot, d in enumerate((2, 6, 1, 7))]
+        for copy in copies:
+            copy.start()
+
+        def project(total, d):
             there = lax.rem(z + d, LAYERS)
-            for half in range(2):
-                arrived(wbuf.at[l, 2 * there + half], wsem.at[l, 2 * there + half])
-            if d:
-                arrived(nbuf.at[l, there], nsem.at[l, there])
             weight = wbuf[l, pl.ds(2 * there, 2)].reshape(WIDE, WIDE)
-            total = total + contract(nbuf[l, there], weight, 1, 0)
+            return total + contract(nbuf[l, there], weight, 1, 0)
+
+        def gathered(d):
+            there = lax.rem(z + d, LAYERS)
+            arrived(nbuf.at[l, there], nsem.at[l, there])
+
+        arrived(wbuf.at[l], wsem.at[l])
+        total = project(x.astype(F32), 0)
+        for d, source, rows, one, two in ((6, behind, early, 1, 2), (2, ahead, late, 7, 6)):
+            gathered(d)
+            far = [onward(source, rows, len(copies), two), onward(source, every, len(copies) + 1, one)]
+            for copy in far:
+                copy.start()
+            copies += far
+        for d in (1, 7, 2, 6, 3, 5, 4):
+            if d not in (2, 6):
+                gathered(d)
+            total = project(total, d)
 
         @pl.when(l > 0)
         def _():
@@ -386,7 +415,8 @@
         xbuf[...] = total.astype(BF16)
         for d in range(1, LAYERS):
             sent(sbuf.at[l, z], ssend.at[d])
-            sent(nbuf.at[l, z], nsend.at[d])
+        for copy in copies:
+            copy.wait_send()
 
         def states_sent(there, carry):
             sent(tbuf.at[l, c], tsend.at[there])
@@ -455,9 +485,11 @@
             dma((4,)),
             dma((2, LAYERS)),
             dma((2, LAYERS)),
-            dma((20,)),
-            dma((LAYERS, BLOCKS)),
-            dma((LAYERS, OWN)),
+            dma((LAYERS, 2, 4)),
+            dma((LAYERS, 2, 4)),
+            dma((LAYERS, 36)),
+            dma((LAYERS,)),
+            dma((LAYERS,)),
         ],
         compiler_params=pltpu.CompilerParams(collective_id=0, has_side_effects=True, vmem_limit_bytes=58 << 20),
     )(hidden_in[0], weight, qkv, decay, lengths)

time: 310 us -> 209 us (0.67)
  Pallas kernels: 302 us -> 201 us
    pallas_call x1, Pallas kernels: 302 us -> 201 us  [shards(): pl.pallas_call(kernel, out_shape=jax.ShapeDtypeStruct((ROWS, half), BF16)...]
where the time goes in v2:
time: 209 us
  Pallas kernels  201 us (96%)
  local copies, waits for them, and re-layouts  4.82 us (2%)
  other arithmetic  2.87 us (1%)
    pallas_call x1, Pallas kernels, shards(): pl.pallas_call(kernel, out_shape=jax.ShapeDtypeStruct((ROWS, half), BF16)...  201 us

profile of v2, /device:TPU:31, one launch (start us, length us, event | category | flops | bytes accessed | tf_op | source)
XLA Modules:
  0.0 208.5 jit_solution(2443024943693090310)
XLA Ops:
  0.0 0.0 copy-start
  0.0 0.9 multiply_exponential_fusion
  0.9 0.1 copy.12
  1.0 0.1 broadcast_in_dim.6
  1.0 0.1 mul.13
  1.1 1.3 pad.4.ld
  2.4 2.0 fusion.wd
  4.4 0.0 copy-done
  4.4 1.5 copy.10
  5.9 200.8 %shard_map.64 = bf16[128,1536]{1,0:T(8,128)(2,1)} custom-call(bf16[128,1536]{1,0:T(8,128)(2,1)} %bitcast.18, bf16[192,1536]{1,0:T(8,128)(2,1)} %fusion.wd, bf16[16,288,96]{2,1,0:T(8,128)(2,1)} %bitcast.16, f32[4,8,128]{2,1,0:T(8,128)} %pad.4.ld, s32[1,4]{1,0:T(1,128)} %lens.1), custom_call_target="tpu_custom_call" | custom-call | tf_op jit(solution)/shard_map/pallas_call | solution.py:450
  206.8 1.8 copy.14
Async XLA Ops:
  0.0 4.4 %copy-start = (bf16[1,16,96,288]{3,2,1,0:T(8,128)(2,1)S(1)}, bf16[1,16,96,288]{3,2,1,0:T(8,128)(2,1)}, u32[]{:S(2)}) copy-start(bf16[1,16,96,288]{3,2,1,0:T(8,128)(2,1)} %param.7) | copy-start | bytes 2654212

commit v3 on v2

--- a/solution.py
+++ b/solution.py
@@ -23,11 +23,12 @@
 
 
 def kernel(
-    hid, wd, qk, ld, lens, out,
-    xbuf, sbuf, nbuf, tbuf, wbuf, qbuf, graw, gbuf, cbuf, mbuf, wst, qst, wsrc, qsrc,
+    hid, qkv, decay, lens, mantissa, exponent, out,
+    xbuf, sbuf, nbuf, tbuf, wbuf, qbuf, graw, gbuf, cbuf, mbuf, allow, wst, qst, wsrc, qsrc,
     bits, ldsend, hsem, sibsend, sibsem, gsem, csend, csem,
     ssend, ssem, tsend, tsem, nsend, nsem, osend, osem,
-    zsend, zsem, psend, psem, rsend, wsem, qsem,
+    zsend, zsem, psend, psem, rsend, wsem, qsem, nsem2,
+    wd, qk, ld, mraw, qraw, draw, eraw, loadsem,
 ):
     z, c, t = lax.axis_index("phase"), lax.axis_index("ctx"), lax.axis_index("tp")
     y = lax.rem(c, 4)
@@ -63,10 +64,41 @@
         return carry
 
     lax.fori_loop(1, BLOCKS, greet_plane, 0)
+
+    loads = [pltpu.make_async_copy(qkv.at[4 * k + y], qraw.at[k], loadsem.at[k]) for k in range(4)]
+    loads += [
+        pltpu.make_async_copy(mantissa, mraw, loadsem.at[4]),
+        pltpu.make_async_copy(decay, draw, loadsem.at[5]),
+        pltpu.make_async_copy(exponent, eraw, loadsem.at[6]),
+    ]
+    for load in loads:
+        load.start()
+    for k in range(4):
+        loads[k].wait()
+        qk[k] = qraw[k].astype(F32).T.astype(BF16)
+    loads[5].wait()
+    flipped = draw[...]
+    for k in range(4):
+        ld[k] = jnp.concatenate([flipped[OWN * k : OWN * k + OWN], jnp.zeros((8 - OWN, ROWS), F32)], axis=0)
+    loads[6].wait()
+    loads[4].wait()
+    power = eraw[...]
+    scale = jnp.full(power.shape, 2.0, F32)
+    for value in range(4):
+        scale = jnp.where(power == value - 3, 2.0 ** (value - 3), scale)
+    spots = (4 * OWN, MODEL // 2)
+    inside = lax.broadcasted_iota(jnp.int32, spots, 1) - HEAD * lax.broadcasted_iota(jnp.int32, spots, 0)
+    spread = ((inside >= 0) & (inside < HEAD)).astype(BF16)
+    scale = contract(scale.astype(BF16), spread, 0, 0)
+    here = lax.broadcasted_iota(jnp.int32, scale.shape, 0) - 2 * c
+    scale = [jnp.sum(jnp.where(here == r, scale, 0.0), axis=0, keepdims=True) for r in range(2)]
+    for r in range(2):
+        part = mraw[HEAD * r : HEAD * r + HEAD].astype(F32) * scale[r]
+        wd[HEAD * r : HEAD * r + HEAD] = part.astype(BF16)
     pl.semaphore_wait(barrier, 2 * (LAYERS + BLOCKS) - 3)
 
-    hid_local = pltpu.make_async_copy(cols(hid, zr), xbuf, hsem)
-    hid_remote = push(cols(hid, zr), xbuf, sibsend.at[6], hsem, (z, c, 1))
+    hid_local = pltpu.make_async_copy(cols(hid, zr), xbuf.at[0], hsem)
+    hid_remote = push(cols(hid, zr), xbuf.at[0], sibsend.at[2], hsem, (z, c, 1))
 
     @pl.when((t == 1) & (zq == 1))
     def _():
@@ -94,15 +126,32 @@
 
     @pl.when(t == 1)
     def _():
-        for k in range(4):
-            push(qk.at[4 * k + y], qsrc.at[k], sibsend.at[k], sibsem.at[k], (z, c, 0)).start()
-        push(wd, wsrc, sibsend.at[4], sibsem.at[4], (z, c, 0)).start()
+        @pl.when(z == 0)
+        def _():
+            for k in range(4):
+                push(qk.at[k], qst.at[0], zsend.at[0, 4 + k], zsem.at[0, 0], (4 + k, c, 0)).start()
+            for k in range(4):
+                push(cols(wd, k), wst.at[0], zsend.at[1, 4 + k], zsem.at[1, 0], (4 + k, c, 0)).start()
+
+        @pl.when(z > 0)
+        def _():
+            push(qk, qsrc, sibsend.at[0], sibsem.at[0], (z, c, 0)).start()
+            push(wd, wsrc, sibsend.at[1], sibsem.at[1], (z, c, 0)).start()
+
         layers(z, c, zq, zr, push, arrived, sent, cols, hid_local, hid_remote, lens, out,
-               xbuf, sbuf, nbuf, tbuf, wbuf, qbuf, graw, gbuf, cbuf, mbuf, bits,
-               gsem, csend, csem, ssend, ssem, tsend, tsem, nsend, nsem, osend, osem, wsem, qsem)
-        for k in range(4):
-            sent(qsrc.at[k], sibsend.at[k])
-        sent(wsrc, sibsend.at[4])
+               xbuf, sbuf, nbuf, tbuf, wbuf, qbuf, graw, gbuf, cbuf, mbuf, allow, bits,
+               gsem, csend, csem, ssend, ssem, tsend, tsem, nsend, nsem, osend, osem, wsem, qsem, nsem2)
+
+        @pl.when(z == 0)
+        def _():
+            for k in range(4):
+                sent(qk.at[k], zsend.at[0, 4 + k])
+                sent(cols(wd, k), zsend.at[1, 4 + k])
+
+        @pl.when(z > 0)
+        def _():
+            sent(qsrc, sibsend.at[0])
+            sent(wsrc, sibsend.at[1])
 
     @pl.when((t == 0) & (zq == 0))
     def _():
@@ -122,18 +171,15 @@
     x4 = c - y
     upper, lower = pl.ds(0, HEAD), pl.ds(HEAD, HEAD)
 
-    def scatter():
+    def scatter(halves):
         for kind in range(2):
-            for half in range(2):
-                if half and kind == 0:
-                    for k in range(4):
-                        arrived(qsrc.at[k], sibsem.at[k])
-                if half and kind == 1:
-                    arrived(wsrc, sibsem.at[4])
+            for half in halves:
+                if half:
+                    arrived(wsrc if kind else qsrc, sibsem.at[kind])
                 for k in range(4):
                     there = 4 * half + k
                     if kind == 0:
-                        src = qsrc.at[k] if half else qk.at[4 * k + y]
+                        src = qsrc.at[k] if half else qk.at[k]
                         dst = qst.at[z]
                     else:
                         src = cols(wsrc if half else wd, k)
@@ -158,9 +204,9 @@
 
     @pl.when(z == 0)
     def _():
-        scatter()
-
-    def step(l, carry):
+        scatter((0,))
+
+    def first_hop(l):
         staged(0, l, qst)
         for yy in range(4):
             push(qst.at[l], qbuf.at[l, y], rsend.at[l, 32 + yy], qsem.at[l], (z, x4 + yy, 1)).start()
@@ -171,10 +217,7 @@
             push(wst.at[l, lower], wbuf.at[l, c, lower], psend.at[l, 1, d], psem.at[l, 1, y],
                  (z, x4 + lax.rem(y + d, 4), 0)).start()
 
-        @pl.when((l == 0) & (z > 0))
-        def _():
-            scatter()
-
+    def second_hop(l):
         for d in range(4):
             across = lax.rem(c + 4 * d, BLOCKS)
             along = x4 + lax.rem(y + d, 4)
@@ -188,12 +231,26 @@
                 src = wbuf.at[l, along, lower] if d else wst.at[l, lower]
                 push(src, wbuf.at[l, along, lower], rsend.at[l, 16 + 4 * d + e], wsem.at[l],
                      (z, lax.rem(c + 4 * e, BLOCKS), 1)).start()
+
+    def step(l, carry):
+        second_hop(l)
+
+        @pl.when(l < LAYERS - 1)
+        def _():
+            first_hop(l + 1)
+
         return carry
+
+    @pl.when(z > 0)
+    def _():
+        scatter((0, 1))
+
+    first_hop(0)
 
     lax.fori_loop(0, LAYERS, step, 0)
     for there in range(LAYERS):
 
-        @pl.when(z != there)
+        @pl.when((z != there) & (z > 0) if there >= 4 else z != there)
         def _():
             sent(qst.at[z], zsend.at[0, there])
             sent(wst.at[z], zsend.at[1, there])
@@ -215,8 +272,8 @@
 
 
 def layers(z, c, zq, zr, push, arrived, sent, cols, hid_local, hid_remote, lens, out,
-           xbuf, sbuf, nbuf, tbuf, wbuf, qbuf, graw, gbuf, cbuf, mbuf, bits,
-           gsem, csend, csem, ssend, ssem, tsend, tsem, nsend, nsem, osend, osem, wsem, qsem):
+           xbuf, sbuf, nbuf, tbuf, wbuf, qbuf, graw, gbuf, cbuf, mbuf, allow, bits,
+           gsem, csend, csem, ssend, ssem, tsend, tsem, nsend, nsem, osend, osem, wsem, qsem, nsem2):
     e1 = lens[0, 0]
     e2 = e1 + lens[0, 1]
     e3 = e2 + lens[0, 2]
@@ -248,31 +305,21 @@
         def _():
             arrived(graw.at[l], gsem.at[l])
 
-    def decays(l, carry):
-        g = graw[l]
-        for s in (1, 2, 4, 8, 16, 32, 64):
-            g = g + jnp.where(lane8 >= s, pltpu.roll(g, s, 1), 0.0)
-        gbuf[l] = g
-        kept = jnp.exp(jnp.broadcast_to(g[:, ROWS - 1 :], (8, ROWS))) * bits[2]
+    g = graw[...].reshape(LAYERS * 8, ROWS)
+    lane = lax.broadcasted_iota(jnp.int32, (LAYERS * 8, ROWS), 1)
+    for s in (1, 2, 4, 8, 16, 32, 64):
+        g = g + jnp.where(lane >= s, pltpu.roll(g, s, 1), 0.0)
+    gbuf[...] = g.reshape(LAYERS, 8, ROWS)
+    for l in range(LAYERS):
+        kept = jnp.exp(jnp.broadcast_to(g[8 * l : 8 * l + 8, ROWS - 1 :], (8, ROWS))) * bits[2]
         cbuf[c, l] = jnp.where(lane8 < HEAD, kept, jnp.broadcast_to(kept[3:4], (8, ROWS)))
-        return carry
-
-    lax.fori_loop(0, LAYERS, decays, 0)
 
     def tell(there, carry):
         push(cbuf.at[c], cbuf.at[c], csend.at[there], csem.at[c], (z, there, 1)).start()
         return carry
 
     lax.fori_loop(c + 1, BLOCKS, tell, 0)
-    allowed = later & (seg_row == seg_col)
-
-    def masks(l, carry):
-        for h in range(OWN):
-            row = jnp.broadcast_to(gbuf[l, h : h + 1], (ROWS, ROWS))
-            mbuf[l, h] = jnp.exp(jnp.where(allowed, row - row.T, -1e30))
-        return carry
-
-    lax.fori_loop(0, LAYERS, masks, 0)
+    allow[...] = jnp.where(later & (seg_row == seg_col), 0.0, -1e30)
 
     @pl.when(zq == 1)
     def _():
@@ -282,11 +329,6 @@
     def _():
         hid_remote.wait_recv()
 
-    def heard(there, carry):
-        arrived(cbuf.at[there], csem.at[there])
-        return carry
-
-    lax.fori_loop(0, c, heard, 0)
     lane96 = lax.broadcasted_iota(jnp.int32, (HEAD, ROWS), 1)
 
     def emit(l):
@@ -294,30 +336,45 @@
 
         @pl.when(self_kept)
         def _():
-            pltpu.make_async_copy(xbuf, cols(out, zr), osem.at[zr]).start()
+            pltpu.make_async_copy(xbuf.at[l + 1], cols(out, zr), osem.at[zr]).start()
 
         @pl.when(jnp.logical_not(self_kept))
         def _():
-            push(xbuf, cols(out, zr), osend, osem.at[zr], (l, c, zq)).start()
+            push(xbuf.at[l + 1], cols(out, zr), osend.at[l], osem.at[zr], (l, c, zq)).start()
 
     def emitted(l):
         self_kept = (zq == 1) & (z == l)
 
         @pl.when(self_kept)
         def _():
-            pltpu.make_async_copy(xbuf, cols(out, zr), osem.at[zr]).wait()
+            pltpu.make_async_copy(xbuf.at[l + 1], cols(out, zr), osem.at[zr]).wait()
 
         @pl.when(jnp.logical_not(self_kept))
         def _():
-            sent(xbuf, osend)
+            sent(xbuf.at[l + 1], osend.at[l])
+
+    def gone(l):
+        for slot in range(10):
+            if slot in (4, 5, 8, 9):
+                sent(nbuf.at[l, z], nsend.at[l, slot])
+            else:
+                sent(nbuf.at[l, z, pl.ds(0, ROWS // 2)], nsend.at[l, slot])
 
     def layer(l, carry):
-        x = xbuf[...]
+        x = xbuf[l]
         xt = x.astype(F32).T
         own_squares = jnp.sum(xt * xt, axis=0, keepdims=True)
         sbuf[l, z] = own_squares
         for d in (4, 3, 5, 2, 6, 1, 7):
-            push(sbuf.at[l, z], sbuf.at[l, z], ssend.at[d], ssem.at[l, z], (lax.rem(z + d, LAYERS), c, 1)).start()
+            push(sbuf.at[l, z], sbuf.at[l, z], ssend.at[l, d], ssem.at[l, z], (lax.rem(z + d, LAYERS), c, 1)).start()
+        for h in range(OWN):
+            row = jnp.broadcast_to(gbuf[l, h : h + 1], (ROWS, ROWS))
+            mbuf[h] = jnp.exp(row - row.T + allow[...])
+
+        @pl.when(l > 0)
+        def _():
+            gone(l - 1)
+
         arrived(qbuf.at[l], qsem.at[l])
         squares = own_squares
         for d in (1, 7, 2, 6, 3, 5, 4):
@@ -325,7 +382,8 @@
             arrived(sbuf.at[l, there], ssem.at[l, there])
             squares = squares + sbuf[l, there]
         xtb = (xt * lax.rsqrt(squares / MODEL + EPSILON)).astype(BF16)
-        raw = [contract(qbuf[l, h], xtb[HEAD * h : HEAD * h + HEAD], 1, 0) for h in range(OWN)]
+        heads = [xtb[HEAD * h : HEAD * h + HEAD] for h in range(OWN)]
+        raw = [contract(qbuf[l, h, HEAD:], heads[h], 1, 0) for h in range(OWN)]
 
         @pl.when(l > 0)
         def _():
@@ -336,9 +394,9 @@
         query_scale = jnp.exp(g) * bits[1]
         keys, values, keyed = [], [], []
         for h in range(OWN):
-            k = jax.nn.silu(raw[h][HEAD : 2 * HEAD]).astype(BF16)
+            k = jax.nn.silu(raw[h][:HEAD]).astype(BF16)
             keys.append(k)
-            values.append(raw[h][2 * HEAD :].astype(BF16))
+            values.append(raw[h][HEAD:].astype(BF16))
             keyed.append((k.astype(F32) * key_scale[h : h + 1]).astype(BF16))
         for p in range(3):
             right = jnp.concatenate([keyed[p], keyed[3][32 * p : 32 * p + 32]], axis=0)
@@ -346,20 +404,24 @@
             tbuf[l, c, HEAD * p : HEAD * p + HEAD] = jnp.where(lane96 < HEAD, both[:HEAD], both[HEAD:]).astype(BF16)
 
         def states_out(there, carry):
-            push(tbuf.at[l, c], tbuf.at[l, c], tsend.at[there], tsem.at[l, c], (z, there, 1)).start()
+            push(tbuf.at[l, c], tbuf.at[l, c], tsend.at[l, there], tsem.at[l, c], (z, there, 1)).start()
             return carry
 
         lax.fori_loop(c + 1, BLOCKS, states_out, 0)
 
         inner, queried = [], []
         for h in range(OWN):
-            q = jax.nn.silu(raw[h][:HEAD]).astype(BF16)
+            q = jax.nn.silu(contract(qbuf[l, h, :HEAD], heads[h], 1, 0)).astype(BF16)
             scores = contract(keys[h], q, 0, 0)
-            weights = (scores * mbuf[l, h]).astype(BF16)
+            weights = (scores * mbuf[h]).astype(BF16)
             inner.append(contract(values[h], weights, 1, 0))
             queried.append((q.astype(F32) * query_scale[h : h + 1]).astype(BF16))
 
         def fold(there, state):
+            @pl.when(l == 0)
+            def _():
+                arrived(cbuf.at[there], csem.at[there])
+
             arrived(tbuf.at[l, there], tsem.at[l, there])
             return tuple(
                 s * cbuf[there, l, p : p + 1] + tbuf[l, there, HEAD * p : HEAD * p + HEAD].astype(F32)
@@ -367,6 +429,7 @@
             )
 
         state = lax.fori_loop(0, c, fold, tuple(jnp.zeros((HEAD, ROWS), F32) for _ in range(3)))
+
         attended = list(inner)
         for p in range(3):
             left = jnp.concatenate([queried[p], jnp.zeros((32, ROWS), BF16)], axis=0)
@@ -376,15 +439,18 @@
             attended[3] = attended[3] + both[:, ROWS:]
         normed = [a * lax.rsqrt(jnp.mean(a * a, axis=0, keepdims=True) + EPSILON) for a in attended]
         nbuf[l, z] = jnp.concatenate(normed, axis=0).T.astype(BF16)
-        def onward(source, rows, slot, d):
+        def onward(source, rows, slot, d, sem=nsem):
             part = nbuf.at[l, source, rows]
-            return push(part, part, nsend.at[slot], nsem.at[l, source], (lax.rem(z + d, LAYERS), c, 1))
+            return push(part, part, nsend.at[l, slot], sem.at[l, source], (lax.rem(z + d, LAYERS), c, 1))
 
         every, early, late = pl.ds(0, ROWS), pl.ds(0, ROWS // 2), pl.ds(ROWS // 2, ROWS // 2)
         behind, ahead = lax.rem(z + 6, LAYERS), lax.rem(z + 2, LAYERS)
-        copies = [onward(z, every, slot, d) for slot, d in enumerate((2, 6, 1, 7))]
-        for copy in copies:
-            copy.start()
+        onward(z, early, 0, 2).start()
+        onward(z, late, 1, 6).start()
+        onward(z, late, 2, 2, nsem2).start()
+        onward(z, early, 3, 6, nsem2).start()
+        onward(z, every, 4, 1).start()
+        onward(z, every, 5, 7).start()
 
         def project(total, d):
             there = lax.rem(z + d, LAYERS)
@@ -395,39 +461,40 @@
             there = lax.rem(z + d, LAYERS)
             arrived(nbuf.at[l, there], nsem.at[l, there])
 
+        for d in range(1, LAYERS):
+            sent(sbuf.at[l, z], ssend.at[l, d])
+
+        def states_sent(there, inner):
+            sent(tbuf.at[l, c], tsend.at[l, there])
+            return inner
+
+        lax.fori_loop(c + 1, BLOCKS, states_sent, 0)
         arrived(wbuf.at[l], wsem.at[l])
         total = project(x.astype(F32), 0)
-        for d, source, rows, one, two in ((6, behind, early, 1, 2), (2, ahead, late, 7, 6)):
-            gathered(d)
-            far = [onward(source, rows, len(copies), two), onward(source, every, len(copies) + 1, one)]
-            for copy in far:
-                copy.start()
-            copies += far
+        for source, rows, slot, two in ((behind, early, 6, 2), (ahead, late, 7, 6)):
+            arrived(nbuf.at[l, source, rows], nsem.at[l, source])
+            onward(source, rows, slot, two).start()
+        for source, rows, slot, one in ((behind, late, 8, 1), (ahead, early, 9, 7)):
+            arrived(nbuf.at[l, source, rows], nsem2.at[l, source])
+            onward(source, every, slot, one).start()
         for d in (1, 7, 2, 6, 3, 5, 4):
             if d not in (2, 6):
                 gathered(d)
             total = project(total, d)
 
-        @pl.when(l > 0)
-        def _():
-            emitted(l - 1)
-
-        xbuf[...] = total.astype(BF16)
-        for d in range(1, LAYERS):
-            sent(sbuf.at[l, z], ssend.at[d])
-        for copy in copies:
-            copy.wait_send()
-
-        def states_sent(there, carry):
-            sent(tbuf.at[l, c], tsend.at[there])
-            return carry
-
-        lax.fori_loop(c + 1, BLOCKS, states_sent, 0)
+        xbuf[l + 1] = total.astype(BF16)
         return carry
 
     lax.fori_loop(0, LAYERS, layer, 0)
     emit(LAYERS - 1)
-    emitted(LAYERS - 1)
+
+    gone(LAYERS - 1)
+
+    def settle(l, carry):
+        emitted(l)
+        return carry
+
+    lax.fori_loop(0, LAYERS, settle, 0)
 
     def told(there, carry):
         sent(cbuf.at[c], csend.at[there])
@@ -437,23 +504,16 @@
 
 
 def shards(hidden_in, qkv_weight, log_decay, lengths, out_mantissa, out_exponent):
-    ctx = lax.axis_index("ctx")
-    exponent = lax.dynamic_slice_in_dim(out_exponent[0], 2 * ctx, 2, 0)
-    scale = jnp.exp2(exponent.astype(F32))
-    scale = jnp.repeat(scale, HEAD, axis=1)[:, None, :]
-    weight = (out_mantissa[0].astype(F32).reshape(2, HEAD, -1) * scale).reshape(2 * HEAD, -1).astype(BF16)
-    qkv = qkv_weight[0].swapaxes(1, 2)
-    decay = jnp.pad(log_decay[0, 0].T.reshape(4, OWN, ROWS), ((0, 0), (0, 8 - OWN), (0, 0)))
     half = hidden_in.shape[2]
     dma = pltpu.SemaphoreType.DMA
     anywhere = pl.BlockSpec(memory_space=pl.ANY)
     outputs = pl.pallas_call(
         kernel,
         out_shape=jax.ShapeDtypeStruct((ROWS, half), BF16),
-        in_specs=[anywhere] * 4 + [pl.BlockSpec(memory_space=pltpu.SMEM)],
+        in_specs=[anywhere] * 3 + [pl.BlockSpec(memory_space=pltpu.SMEM)] + [anywhere] * 2,
         out_specs=anywhere,
         scratch_shapes=[
-            pltpu.VMEM((ROWS, WIDE), BF16),
+            pltpu.VMEM((LAYERS + 1, ROWS, WIDE), BF16),
             pltpu.VMEM((LAYERS, LAYERS, 1, ROWS), F32),
             pltpu.VMEM((LAYERS, LAYERS, ROWS, WIDE), BF16),
             pltpu.VMEM((LAYERS, BLOCKS, 3 * HEAD, ROWS), BF16),
@@ -462,7 +522,8 @@
             pltpu.VMEM((LAYERS, 8, ROWS), F32),
             pltpu.VMEM((LAYERS, 8, ROWS), F32),
             pltpu.VMEM((BLOCKS, LAYERS, 8, ROWS), F32),
-            pltpu.VMEM((LAYERS, OWN, ROWS, ROWS), F32),
+            pltpu.VMEM((OWN, ROWS, ROWS), F32),
+            pltpu.VMEM((ROWS, ROWS), F32),
             pltpu.VMEM((LAYERS, 2 * HEAD, WIDE), BF16),
             pltpu.VMEM((LAYERS, 3 * HEAD, HEAD), BF16),
             pltpu.VMEM((2 * HEAD, half), BF16),
@@ -470,18 +531,18 @@
             pltpu.VMEM((3, 8, ROWS), F32),
             dma((4,)),
             dma,
-            dma((7,)),
-            dma((5,)),
+            dma((3,)),
+            dma((2,)),
             dma((LAYERS,)),
             dma((BLOCKS,)),
             dma((BLOCKS,)),
+            dma((LAYERS, LAYERS)),
+            dma((LAYERS, LAYERS)),
+            dma((LAYERS, BLOCKS)),
+            dma((LAYERS, BLOCKS)),
+            dma((LAYERS, 10)),
+            dma((LAYERS, LAYERS)),
             dma((LAYERS,)),
-            dma((LAYERS, LAYERS)),
-            dma((BLOCKS,)),
-            dma((LAYERS, BLOCKS)),
-            dma((LAYERS,)),
-            dma((LAYERS, LAYERS)),
-            dma,
             dma((4,)),
             dma((2, LAYERS)),
             dma((2, LAYERS)),
@@ -490,9 +551,18 @@
             dma((LAYERS, 36)),
             dma((LAYERS,)),
             dma((LAYERS,)),
+            dma((LAYERS, LAYERS)),
+            pltpu.VMEM((2 * HEAD, half), BF16),
+            pltpu.VMEM((4, 3 * HEAD, HEAD), BF16),
+            pltpu.VMEM((4, 8, ROWS), F32),
+            pltpu.VMEM((2 * HEAD, half), BF16),
+            pltpu.VMEM((4, HEAD, 3 * HEAD), BF16),
+            pltpu.VMEM((4 * OWN, ROWS), F32),
+            pltpu.VMEM((4 * OWN, 2 * OWN * 4), jnp.int32),
+            dma((7,)),
         ],
         compiler_params=pltpu.CompilerParams(collective_id=0, has_side_effects=True, vmem_limit_bytes=58 << 20),
-    )(hidden_in[0], weight, qkv, decay, lengths)
+    )(hidden_in[0], qkv_weight[0], log_decay[0, 0].T, lengths, out_mantissa[0], out_exponent[0].T)
     return outputs[None, None]
 
 

time: 209 us -> 208 us (level)
  Pallas kernels: 201 us -> 206 us
  local copies, waits for them, and re-layouts: 4.82 us -> 1.77 us
  other arithmetic: 2.87 us -> 0 us
    pallas_call x1, Pallas kernels: 201 us -> 206 us  [shards(): pl.pallas_call(kernel, out_shape=jax.ShapeDtypeStruct((ROWS, half), BF16)...]
where the time goes in v3:
time: 208 us
  Pallas kernels  206 us (99%)
    pallas_call x1, Pallas kernels, shards(): pl.pallas_call(kernel, out_shape=jax.ShapeDtypeStruct((ROWS, half), BF16)...  206 us

profile of v3, /device:TPU:31, one launch (start us, length us, event | category | flops | bytes accessed | tf_op | source)
XLA Modules:
  0.0 207.9 jit_solution(9758748145810206074)
XLA Ops:
  0.0 206.1 %shard_map.64 = bf16[128,1536]{1,0:T(8,128)(2,1)} custom-call(bf16[128,1536]{1,0:T(8,128)(2,1)} %bitcast.13, bf16[16,96,288]{2,1,0:T(8,128)(2,1)} %bitcast.11, f32[16,128]{1,0:T(8,128)} %bitcast.14, s32[1,4]{1,0:T(1,128)} %lens.1, bf16[192,1536]{1,0:T(8,128)(2,1)} %bitcast.12, s32[16,32]{1,0:T(8,128)} %bitcast.15), custom_call_target="tpu_custom_call" | custom-call | tf_op jit(solution)/shard_map/pallas_call | solution.py:510
  206.1 1.8 copy.8

commit v4 on v3

--- a/solution.py
+++ b/solution.py
@@ -224,7 +224,7 @@
             if d:
                 arrived(wbuf.at[l, across, upper], psem.at[l, 0, across // 4])
                 arrived(wbuf.at[l, along, lower], psem.at[l, 1, along - x4])
-            for e in (1, 3, 2, 0):
+            for e in (2, 1, 3, 0):
                 src = wbuf.at[l, across, upper] if d else wst.at[l, upper]
                 push(src, wbuf.at[l, across, upper], rsend.at[l, 4 * d + e], wsem.at[l],
                      (z, x4 + lax.rem(y + e, 4), 1)).start()

time: 208 us -> 208 us (level)
  no operation moved by 1% of the time
where the time goes in v4:
time: 208 us
  Pallas kernels  206 us (99%)
    pallas_call x1, Pallas kernels, shards(): pl.pallas_call(kernel, out_shape=jax.ShapeDtypeStruct((ROWS, half), BF16)...  206 us

profile of v4, /device:TPU:31, one launch (start us, length us, event | category | flops | bytes accessed | tf_op | source)
XLA Modules:
  0.0 208.2 jit_solution(4899747413711632594)
XLA Ops:
  0.0 206.4 %shard_map.64 = bf16[128,1536]{1,0:T(8,128)(2,1)} custom-call(bf16[128,1536]{1,0:T(8,128)(2,1)} %bitcast.13, bf16[16,96,288]{2,1,0:T(8,128)(2,1)} %bitcast.11, f32[16,128]{1,0:T(8,128)} %bitcast.14, s32[1,4]{1,0:T(1,128)} %lens.1, bf16[192,1536]{1,0:T(8,128)(2,1)} %bitcast.12, s32[16,32]{1,0:T(8,128)} %bitcast.15), custom_call_target="tpu_custom_call" | custom-call | tf_op jit(solution)/shard_map/pallas_call | solution.py:510
  206.4 1.8 copy.8
